TPU v7x, 32 devices: a whole 2x2x4 slice. The times are simulated.
32 devices in a mesh: row: 8 (over z, x), col: 4 (over y, core).
Axes of the slice: x: 2, y: 2, z: 4, core: 2. Of those that a mesh axis runs over, the one named last changes fastest.
Arguments:
- interaction: bfloat16 [5, 8192, 8192], P(None, 'row', 'col'), may hold values from -0.0390625 to 0.0390625
- history_currents: bfloat16 [4, 8192, 512], P(None, ('col', 'row')), may hold values from -5 to 5
- incident: float32 [2, 8192, 512], P(None, ('row', 'col')), may hold values from -4 to 4
- load_gain: float32 [8192], P('row'), may hold values from 0.5 to 1.5
- load_cubic: float32 [8192], P('row'), may hold values from 0.005 to 0.04
- delays: int32 [8, 4, 5], P('row', 'col'), may hold values from 1 to 4
- tile_map: int32 [8, 4], P('row', 'col'), may hold values 0 or 1
Outputs:
- currents: bfloat16 [2, 8192, 512], P(None, ('row', 'col'))
Inputs may be any that keep to these rules, and one draw needn't show every extreme that they name: Slot k of tile (r, c) reads the current of delays[r, c, k] steps before the marched step.
All inputs are finite; a program needn't handle non-finite values. No bound on the sum of `tile_map` on one device may be relied on, other than what follows from the above.
Results may differ from a plain program's by a relative error of at most 0.0024.
Values may be sent and summed in bfloat16 or wider, within the bound.
No kernel may reach another device: no remote copies, remote signals or barrier semaphores. Data moves between devices by JAX's collectives and lax.ppermute only.
A program may use at most 128 MiB of HBM per device.

v0:
```python
import jax
import jax.numpy as jnp
from jax import lax
from jax.sharding import PartitionSpec as P

K = 5
H = 4
STEPS = 2


def shifted_2(value, axis, steps):
    count = lax.axis_size(axis)
    pairs = [(source, (source + steps) % count) for source in range(count)]
    return lax.ppermute(value, axis, pairs)


def route_share(current, fanout):
    cols_count = lax.axis_size("col")
    col_index = lax.axis_index("col")
    row_index = lax.axis_index("row")
    bit_count = (cols_count - 1).bit_length()
    moving = current
    for bit in range(bit_count):
        shifted = shifted_2(moving, "row", -(fanout << bit))
        moving = jnp.where(col_index >> bit & 1 == 1, shifted, moving)
    band = row_index // fanout
    for bit in range(bit_count):
        shifted = shifted_2(moving, "col", 1 << bit)
        moving = jnp.where(band >> bit & 1 == 1, shifted, moving)
    gathered = lax.all_gather(moving, "row", axis=0, tiled=True)
    share_rows = moving.shape[0]
    waves = moving.shape[1]
    grid = gathered.reshape(cols_count, fanout, share_rows, waves)
    order = (col_index - jnp.arange(cols_count, dtype=jnp.int32)) % cols_count
    picked = jnp.take(grid, order, axis=0)
    return jnp.swapaxes(picked, 0, 1).reshape(cols_count * fanout * share_rows, waves)


def per_device(interaction, history_currents, incident, load_gain, load_cubic, delays, tile_map):
    fanout = lax.axis_size("row") // lax.axis_size("col")
    col_index = lax.axis_index("col")
    block_obs = interaction.shape[1]
    share_rows = incident.shape[1]
    waves = incident.shape[2]
    past = lax.all_gather(history_currents, "row", axis=1, tiled=True)
    buffer = jnp.concatenate([past, jnp.zeros((STEPS,) + past.shape[1:], jnp.bfloat16)], axis=0)
    weight = tile_map[0, 0].astype(jnp.float32)
    start = col_index * share_rows
    gain_share = lax.dynamic_slice_in_dim(load_gain, start, share_rows, 0)
    cubic_share = lax.dynamic_slice_in_dim(load_cubic, start, share_rows, 0)
    results = []
    for instant in range(STEPS):
        partial_value = jnp.zeros((block_obs, waves), jnp.float32)
        for slot_number in range(K):
            position = H + instant - delays[0, 0, slot_number]
            source = lax.dynamic_index_in_dim(buffer, position, 0, keepdims=False)
            partial_value = partial_value + jnp.dot(
                interaction[slot_number], source, preferred_element_type=jnp.float32
            )
        summands = -(partial_value * weight)
        own_rows = lax.dynamic_slice_in_dim(summands, start, share_rows, 0) + incident[instant]
        summands = lax.dynamic_update_slice_in_dim(summands, own_rows, start, 0)
        more = instant + 1 < STEPS
        field = lax.psum_scatter(summands, "col", scatter_dimension=0, tiled=True)
        current = (
            gain_share[:, None] * field - cubic_share[:, None] * field * field * field
        ).astype(jnp.bfloat16)
        results.append(current)
        if more:
            buffer = buffer.at[H + instant].set(route_share(current, fanout))
    return jnp.stack(results)


def solution(mesh):
    placed = (
        P(None, "row", "col"),
        P(None, ("col", "row"), None),
        P(None, ("row", "col"), None),
        P("row"),
        P("row"),
        P("row", "col", None),
        P("row", "col"),
    )
    return jax.shard_map(
        per_device,
        mesh=mesh,
        in_specs=placed,
        out_specs=P(None, ("row", "col"), None),
        check_vma=False,
    )
```

profile of v0, /device:TPU:0, one launch (start us, length us, event | category | flops | bytes accessed | tf_op | source)
XLA Modules:
  0.0 369.9 jit_solution(18213386568255099205)
XLA Ops:
  6.5 0.0 all-gather.3.cloned.1.call-start
  6.5 0.7 all-gather.3.cloned.1.call-update
  7.3 0.0 reduce-scatter.3.cloned.1.call-start
  7.3 1.5 fusion.85
  15.6 2.1 fusion.84
  17.6 0.2 copy.12
  17.9 119.3 %all-gather.3.cloned.1.call-done = bf16[4,2048,512]{2,1,0:T(8,128)(2,1)} async-done(((bf16[4,256,512]{2,1,0:T(8,128)(2,1)}), bf16[4,2048,512]{2,1,0:T(8,128)(2,1)}) %all-gather.3.cloned.1.call-update) | async-done | bytes 8388624 | tf_op jit(solution)/shard_map/all_gather | solution.py:45
  137.2 0.0 copy-start
  137.2 5.4 %fusion.10 = f32[512,1024]{1,0:T(8,128)S(1)} fusion(bf16[5,1024,2048]{2,1,0:T(8,128)(2,1)} %param.9, s32[]{:T(128)S(6)} %select_n.114, bf16[4,2048,512]{2,1,0:T(8,128)(2,1)} %all-gather.3.cloned.1.call-done), kind=kOutput, calls=%fused_computation.11 | convolution fusion | flops 2147483648 | bytes 14680068 | tf_op jit(solution)/shard_map/dot_general | solution.py:57
  142.5 0.0 copy-done
  142.6 4.6 %fusion.14 = f32[512,1024]{1,0:T(8,128)S(1)} fusion(bf16[5,1024,2048]{2,1,0:T(8,128)(2,1)} %param.9, s32[]{:T(128)S(6)} %select_n.113, bf16[4,2048,512]{2,1,0:T(8,128)(2,1)S(1)} %copy-done), kind=kOutput, calls=%fused_computation.15 | convolution fusion | flops 2147483648 | bytes 14680068 | tf_op jit(solution)/shard_map/dot_general | solution.py:57
  147.2 4.6 %fusion.2 = f32[512,1024]{1,0:T(8,128)S(1)} fusion(bf16[5,1024,2048]{2,1,0:T(8,128)(2,1)} %param.9, s32[]{:T(128)S(6)} %select_n.116, bf16[4,2048,512]{2,1,0:T(8,128)(2,1)S(1)} %copy-done), kind=kOutput, calls=%fused_computation.3 | convolution fusion | flops 2147483648 | bytes 14680068 | tf_op jit(solution)/shard_map/dot_general | solution.py:57
  151.8 4.6 %fusion.6 = f32[512,1024]{1,0:T(8,128)S(1)} fusion(bf16[5,1024,2048]{2,1,0:T(8,128)(2,1)} %param.9, s32[]{:T(128)S(6)} %select_n.115, bf16[4,2048,512]{2,1,0:T(8,128)(2,1)S(1)} %copy-done), kind=kOutput, calls=%fused_computation.7 | convolution fusion | flops 2147483648 | bytes 14680068 | tf_op jit(solution)/shard_map/dot_general | solution.py:57
  156.4 5.1 %multiply_negate_fusion.1 = f32[512,1024]{1,0:T(8,128)S(1)} fusion(f32[512,1024]{1,0:T(8,128)S(1)} %fusion.2, f32[512,1024]{1,0:T(8,128)S(1)} %fusion.6, f32[512,1024]{1,0:T(8,128)S(1)} %fusion.10, f32[512,1024]{1,0:T(8,128)S(1)} %fusion.14, bf16[5,1024,2048]{2,1,0:T(8,128)(2,1)} %param.9, s32[]{:T(128)S(6)} %select_n.112, ...), kind=kOutput, calls=%fused_computation.48 | convolution fusion | flops 2150629376 | bytes 23069188 | tf_op jit(solution)/shard_map/dot_general | solution.py:57
  161.6 0.2 copy.14
  161.8 0.1 fusion.64
  161.9 0.0 copy-start.3
  161.9 1.3 copy-done.3
  163.3 0.0 reduce-scatter.3.cloned.1.call-update
  163.3 0.0 all-gather.5.cloned.1.call-start
  163.3 0.8 dynamic_slice.43
  164.1 0.8 dynamic_slice.50
  164.9 0.0 copy-start.5
  164.9 28.2 %reduce-scatter.3.cloned.1.call-done = f32[256,512]{0,1:T(8,128)} async-done(((f32[1024,512]{0,1:T(8,128)}), f32[256,512]{0,1:T(8,128)}) %reduce-scatter.3.cloned.1.call-update) | async-done | bytes 524304 | tf_op jit(solution)/shard_map/reduce_scatter | solution.py:64
  193.0 1.1 fusion.60
  194.2 3.4 collective-permute-start
  197.6 5.6 %collective-permute-done = bf16[256,512]{0,1:T(8,128)(2,1)S(1)} collective-permute-done((bf16[256,512]{0,1:T(8,128)(2,1)S(1)}, bf16[256,512]{0,1:T(8,128)(2,1)S(1)}, u32[]{:S(2)}, u32[]{:S(2)}) %collective-permute-start) | collective-permute-done | bytes 262176 | tf_op jit(solution)/shard_map/ppermute | solution.py:14
  203.1 1.2 broadcast_select_fusion.1
  204.3 1.6 collective-permute-start.1
  205.9 12.1 %collective-permute-done.1 = bf16[256,512]{0,1:T(8,128)(2,1)S(1)} collective-permute-done((bf16[256,512]{0,1:T(8,128)(2,1)S(1)}, bf16[256,512]{0,1:T(8,128)(2,1)S(1)}, u32[]{:S(2)}, u32[]{:S(2)}) %collective-permute-start.1) | collective-permute-done | bytes 262176 | tf_op jit(solution)/shard_map/ppermute | solution.py:14
  218.1 0.1 collective-permute-start.2
  218.2 5.8 %collective-permute-done.2 = bf16[256,512]{0,1:T(8,128)(2,1)S(1)} collective-permute-done((bf16[256,512]{0,1:T(8,128)(2,1)S(1)}, bf16[256,512]{0,1:T(8,128)(2,1)S(1)}, u32[]{:S(2)}, u32[]{:S(2)}) %collective-permute-start.2) | collective-permute-done | bytes 262176 | tf_op jit(solution)/shard_map/ppermute | solution.py:14
  224.0 0.6 collective-permute-start.3
  224.6 5.9 %collective-permute-done.3 = bf16[256,512]{0,1:T(8,128)(2,1)S(1)} collective-permute-done((bf16[256,512]{0,1:T(8,128)(2,1)S(1)}, bf16[256,512]{0,1:T(8,128)(2,1)S(1)}, u32[]{:S(2)}, u32[]{:S(2)}) %collective-permute-start.3) | collective-permute-done | bytes 262176 | tf_op jit(solution)/shard_map/ppermute | solution.py:14
  230.4 0.8 broadcast_select_fusion.4
  231.2 0.0 all-gather.5.cloned.1.call-update
  231.2 0.0 reduce-scatter.5.cloned.1.call-start
  237.4 0.0 copy-done.5
  237.4 0.2 copy.13
  237.7 9.1 %concatenate.5 = bf16[6,2048,512]{2,1,0:T(8,128)(2,1)} pad(bf16[4,2048,512]{2,1,0:T(8,128)(2,1)} %all-gather.3.cloned.1.call-done, bf16[]{:T(256)} %constant.132.clone.1), padding=0_2x0_0x0_0 | pad | bytes 20971522 | tf_op jit(solution)/shard_map/concatenate | solution.py:46
  246.7 35.8 %all-gather.5.cloned.1.call-done = bf16[2048,512]{0,1:T(8,128)(2,1)} async-done(((bf16[256,512]{0,1:T(8,128)(2,1)}), bf16[2048,512]{0,1:T(8,128)(2,1)}) %all-gather.5.cloned.1.call-update) | async-done | bytes 2097168 | tf_op jit(solution)/shard_map/all_gather | solution.py:30
  282.5 4.5 %reshape.133 = bf16[4,2,256,512]{2,1,0,3:T(2,128)(2,1)} reshape(bf16[2048,512]{0,1:T(8,128)(2,1)} %all-gather.5.cloned.1.call-done) | data formatting | bytes 4194304 | tf_op jit(solution)/shard_map/reshape | solution.py:33
  287.0 7.8 %gather_fusion = bf16[4,2,256,512]{2,1,3,0:T(2,128)(2,1)S(1)} fusion(bf16[4,2,256,512]{2,1,0,3:T(2,128)(2,1)} %reshape.133, s32[1024]{0:T(1024)S(1)} %pad_clamp_fusion), kind=kCustom, calls=%fused_computation | custom fusion | bytes 4194320 | tf_op jit(solution)/shard_map/jit(_take)/gather | solution.py:35
  294.8 3.2 fusion.50
  298.0 4.9 %copy.9 = bf16[2,4,256,512]{3,2,1,0:T(8,128)(2,1)S(1)} copy(bf16[2,4,256,512]{2,0,3,1:T(2,128)(2,1)} %fusion.50) | data formatting | bytes 4194304 | tf_op jit(solution)/shard_map/jit(_take)/select_n | solution.py:35
  303.0 1.5 constant_dynamic-update-slice_fusion
  304.5 5.3 %fusion.4 = f32[512,1024]{1,0:T(8,128)S(1)} fusion(bf16[5,1024,2048]{2,1,0:T(8,128)(2,1)} %param.9, bf16[6,2048,512]{2,1,0:T(8,128)(2,1)} %constant_dynamic-update-slice_fusion, s32[]{:T(128)S(6)} %select_n.135), kind=kOutput, calls=%fused_computation.5 | convolution fusion | flops 2147483648 | bytes 8388612 | tf_op jit(solution)/shard_map/dot_general | solution.py:57
  309.9 1.1 copy-done.1
  310.9 4.6 %fusion.8 = f32[512,1024]{1,0:T(8,128)S(1)} fusion(bf16[5,1024,2048]{2,1,0:T(8,128)(2,1)} %param.9, bf16[6,2048,512]{2,1,0:T(8,128)(2,1)S(1)} %copy-done.1, s32[]{:T(128)S(6)} %select_n.134), kind=kOutput, calls=%fused_computation.9 | convolution fusion | flops 2147483648 | bytes 8388612 | tf_op jit(solution)/shard_map/dot_general | solution.py:57
  315.5 4.6 %fusion.12 = f32[512,1024]{1,0:T(8,128)S(1)} fusion(bf16[5,1024,2048]{2,1,0:T(8,128)(2,1)} %param.9, bf16[6,2048,512]{2,1,0:T(8,128)(2,1)S(1)} %copy-done.1, s32[]{:T(128)S(6)} %select_n.133), kind=kOutput, calls=%fused_computation.13 | convolution fusion | flops 2147483648 | bytes 8388612 | tf_op jit(solution)/shard_map/dot_general | solution.py:57
  320.2 4.6 %fusion.16 = f32[512,1024]{1,0:T(8,128)S(1)} fusion(bf16[5,1024,2048]{2,1,0:T(8,128)(2,1)} %param.9, bf16[6,2048,512]{2,1,0:T(8,128)(2,1)S(1)} %copy-done.1, s32[]{:T(128)S(6)} %select_n.132), kind=kOutput, calls=%fused_computation.17 | convolution fusion | flops 2147483648 | bytes 8388612 | tf_op jit(solution)/shard_map/dot_general | solution.py:57
  324.8 4.9 %multiply_negate_fusion = f32[512,1024]{1,0:T(8,128)S(1)} fusion(f32[512,1024]{1,0:T(8,128)S(1)} %fusion.4, f32[512,1024]{1,0:T(8,128)S(1)} %fusion.8, f32[512,1024]{1,0:T(8,128)S(1)} %fusion.16, f32[512,1024]{1,0:T(8,128)S(1)} %fusion.12, bf16[5,1024,2048]{2,1,0:T(8,128)(2,1)} %param.9, bf16[6,2048,512]{2,1,0:T(8,128)(2,1)S(1)} %copy-done.1, ...), kind=kOutput, calls=%fused_computation.47 | convolution fusion | flops 2150629376 | bytes 16777732 | tf_op jit(solution)/shard_map/dot_general | solution.py:57
  329.7 0.2 copy.16
  329.9 0.0 copy-start.4
  329.9 0.1 fusion.63
  330.0 0.0 copy-start.2
  330.0 1.3 copy-done.2
  331.4 0.0 reduce-scatter.5.cloned.1.call-update
  331.4 0.0 copy-done.4
  331.4 0.1 fusion.86
  331.5 29.7 %reduce-scatter.5.cloned.1.call-done = f32[256,512]{0,1:T(8,128)} async-done(((f32[1024,512]{0,1:T(8,128)}), f32[256,512]{0,1:T(8,128)}) %reduce-scatter.5.cloned.1.call-update) | async-done | bytes 524304 | tf_op jit(solution)/shard_map/reduce_scatter | solution.py:64
  361.2 1.1 fusion.65
  362.3 0.1 pad_maximum_fusion
  362.4 1.0 copy.11
  (6 shorter events, 0.1 us)
Async XLA Ops:
  6.5 130.7 %all-gather.3.cloned.1.call-start = ((), (), s32[]{:S(2)}) async-start(), calls=%async_computation.2 | async-start | bytes 9437184 | tf_op jit(solution)/shard_map/all_gather | solution.py:45
  7.3 185.8 %reduce-scatter.3.cloned.1.call-start = ((), (), s32[]{:S(2)}) async-start(), calls=%async_computation.3 | async-start | bytes 2621440 | tf_op jit(solution)/shard_map/reduce_scatter | solution.py:64
  137.2 5.4 %copy-start = (bf16[4,2048,512]{2,1,0:T(8,128)(2,1)S(1)}, bf16[4,2048,512]{2,1,0:T(8,128)(2,1)}, u32[]{:S(2)}) copy-start(bf16[4,2048,512]{2,1,0:T(8,128)(2,1)} %all-gather.3.cloned.1.call-done) | copy-start | bytes 25165828
  161.9 1.3 copy-start.3
  163.3 119.2 %all-gather.5.cloned.1.call-start = ((), (), s32[]{:S(2)}) async-start(), calls=%async_computation.4 | async-start | bytes 2359296 | tf_op jit(solution)/shard_map/all_gather | solution.py:30
  164.9 72.5 %copy-start.5 = (f32[1,256,512]{2,1,0:T(8,128)S(1)}, f32[1,256,512]{2,1,0:T(8,128)}, u32[]{:S(2)}) copy-start(f32[1,256,512]{2,1,0:T(8,128)} %get-tuple-element.17) | copy-start | bytes 1572868
  194.2 9.0 %collective-permute-start = (bf16[256,512]{0,1:T(8,128)(2,1)S(1)}, bf16[256,512]{0,1:T(8,128)(2,1)S(1)}, u32[]{:S(2)}, u32[]{:S(2)}) collective-permute-start(bf16[256,512]{0,1:T(8,128)(2,1)S(1)} %fusion.60), channel_id=1, source_target_pairs={{0,24},{4,28},{8,0},{12,4},{16,8},{20,12},{24,16},{28,20},{1,25},{... | collective-permute-start | bytes 786440 | tf_op jit(solution)/shard_map/ppermute | solution.py:14
  204.3 13.8 %collective-permute-start.1 = (bf16[256,512]{0,1:T(8,128)(2,1)S(1)}, bf16[256,512]{0,1:T(8,128)(2,1)S(1)}, u32[]{:S(2)}, u32[]{:S(2)}) collective-permute-start(bf16[256,512]{0,1:T(8,128)(2,1)S(1)} %broadcast_select_fusion.1), channel_id=1, source_target_pairs={{0,16},{4,20},{8,24},{12,28},{16,0},{20,4},{24,8},{28,12},{1,17},{... | collective-permute-start | bytes 786440 | tf_op jit(solution)/shard_map/ppermute | solution.py:14
  218.1 5.8 %collective-permute-start.2 = (bf16[256,512]{0,1:T(8,128)(2,1)S(1)}, bf16[256,512]{0,1:T(8,128)(2,1)S(1)}, u32[]{:S(2)}, u32[]{:S(2)}) collective-permute-start(bf16[256,512]{0,1:T(8,128)(2,1)S(1)} %broadcast_select_fusion.2), channel_id=1, source_target_pairs={{0,1},{1,2},{2,3},{3,0},{4,5},{5,6},{6,7},{7,4},{8,9},{9,10},{10,1... | collective-permute-start | bytes 786440 | tf_op jit(solution)/shard_map/ppermute | solution.py:14
  224.0 6.4 %collective-permute-start.3 = (bf16[256,512]{0,1:T(8,128)(2,1)S(1)}, bf16[256,512]{0,1:T(8,128)(2,1)S(1)}, u32[]{:S(2)}, u32[]{:S(2)}) collective-permute-start(bf16[256,512]{0,1:T(8,128)(2,1)S(1)} %broadcast_select_fusion.3), channel_id=1, source_target_pairs={{0,2},{1,3},{2,0},{3,1},{4,6},{5,7},{6,4},{7,5},{8,10},{9,11},{10,... | collective-permute-start | bytes 786440 | tf_op jit(solution)/shard_map/ppermute | solution.py:14
  231.2 130.0 %reduce-scatter.5.cloned.1.call-start = ((), (), s32[]{:S(2)}) async-start(), calls=%async_computation.5 | async-start | bytes 2621440 | tf_op jit(solution)/shard_map/reduce_scatter | solution.py:64
  304.5 6.4 %copy-start.1 = (bf16[6,2048,512]{2,1,0:T(8,128)(2,1)S(1)}, bf16[6,2048,512]{2,1,0:T(8,128)(2,1)}, u32[]{:S(2)}) copy-start(bf16[6,2048,512]{2,1,0:T(8,128)(2,1)} %constant_dynamic-update-slice_fusion) | copy-start | bytes 37748740
  329.9 1.5 copy-start.4
  330.0 1.3 copy-start.2
Sparse Core Ops, SparseCore 0:
  9.5 127.5 all-gather.2
  163.4 29.5 reduce-scatter.2
  231.3 51.1 all-gather.4
  331.5 29.6 reduce-scatter.4
where the time goes:
time: 371 us; the launch traced here: 370 us
  waiting for transfers between devices  243 us (65%)
  matrix products  48.4 us (13%)
  local copies, waits for them, and re-layouts  38.6 us (10%)
  between operations  26.3 us (7%)
  other arithmetic  7.85 us (2%)
  starting transfers between devices  5.76 us (2%)
    all_gather x1, waiting for transfers between devices, per_device(): past = lax.all_gather(history_currents, 'row', axis=1, tiled=True)  119 us
    reduce_scatter x2, waiting for transfers between devices, per_device(): field = lax.psum_scatter(summands, 'col', scatter_dimension=0, tiled=True)  57.9 us
    dot_general x10, matrix products, per_device(): jnp.dot(interaction[slot_number], source, preferred_element_type=jnp.floa...  48.4 us
    all_gather x1, waiting for transfers between devices, route_share(): gathered = lax.all_gather(moving, 'row', axis=0, tiled=True)  35.8 us
    ppermute x4, waiting for transfers between devices, shifted_2(): return lax.ppermute(value, axis, pairs)  29.4 us
    concatenate x1, local copies, waits for them, and re-layouts, per_device(): jnp.concatenate([past, jnp.zeros((STEPS,) + past.shape[1:], jnp.bfloat16)...  9.07 us
    gather x1, local copies, waits for them, and re-layouts, route_share(): picked = jnp.take(grid, order, axis=0)  7.8 us
  transfers between devices with their start and end apart: 8, of which 8 were waited for; matrix products, arithmetic and copies ran while one was open for 4% of the time, Pallas kernels for 0%

commit v1 on v0

v1 whole, which is shorter than its diff:
```python
import functools

import jax
import jax.numpy as jnp
from jax import lax
from jax.experimental import pallas as pl
from jax.experimental.pallas import tpu as pltpu
from jax.sharding import PartitionSpec as P

BOTH = ("row", "col")
VMEM_BYTES = 48 * 1024 * 1024


def split_waves(waves):
    unit = 128
    if waves % unit or waves < 2 * unit:
        return [(0, waves)]
    half = (waves // unit + 1) // 2 * unit
    return [(0, half), (half, waves)]


def past_kernel(slots, depth, pieces, scalars, matrix, *refs):
    sources = refs[:pieces]
    incident, first_out, second_out, held, total, arrived = refs[pieces:]
    step = pl.program_id(0)
    waves = first_out.shape[1]
    share = incident.shape[1]

    def fetch(number, place):
        for which in range(pieces):
            @pl.when(number == which)
            def _():
                pltpu.make_async_copy(sources[which], held.at[place], arrived.at[place]).start()

    @pl.when(step == 0)
    def _():
        fetch(0, 0)
        total[...] = jnp.zeros_like(total)

    place = lax.rem(step, 2)

    @pl.when(step + 1 < pieces)
    def _():
        fetch(step + 1, 1 - place)

    pltpu.make_async_copy(sources[0], held.at[place], arrived.at[place]).wait()
    left = jnp.concatenate([matrix[slot] for slot in range(slots)], axis=1)
    right = []
    for slot in range(slots):
        delay = scalars[slot]
        now = held[place, depth - delay]
        later = held[place, jnp.minimum(depth + 1 - delay, depth - 1)]
        later = jnp.where(delay >= 2, later, jnp.zeros_like(later))
        right.append(jnp.concatenate([now, later], axis=1))
    right = jnp.concatenate(right, axis=0)
    total[...] += jnp.dot(left, right, preferred_element_type=jnp.float32)

    @pl.when(step == pieces - 1)
    def _():
        weight = -scalars[slots].astype(jnp.float32)
        first_out[...] = weight * total[:, :waves]
        second_out[...] = weight * total[:, waves:]
        own = pl.ds(pl.multiple_of(scalars[slots + 1], share), share)
        first_out[own, :] += incident[0]
        second_out[own, :] += incident[1]


def past_call(scalars, matrix, sources, incident):
    slots, rows, _ = matrix.shape
    depth, share_src, waves = sources[0].shape
    pieces = len(sources)
    flops = 2 * slots * rows * share_src * pieces * waves * 2
    return pl.pallas_call(
        functools.partial(past_kernel, slots, depth, pieces),
        out_shape=[jax.ShapeDtypeStruct((rows, waves), jnp.float32)] * 2,
        grid_spec=pltpu.PrefetchScalarGridSpec(
            num_scalar_prefetch=1,
            grid=(pieces,),
            in_specs=[pl.BlockSpec((slots, rows, share_src), lambda step, held: (0, 0, held[slots + 2 + step]))]
            + [pl.BlockSpec(memory_space=pl.ANY)] * pieces
            + [pl.BlockSpec(incident.shape, lambda step, held: (0, 0, 0))],
            out_specs=[pl.BlockSpec((rows, waves), lambda step, held: (0, 0))] * 2,
            scratch_shapes=[
                pltpu.VMEM((2, depth, share_src, waves), jnp.bfloat16),
                pltpu.VMEM((rows, 2 * waves), jnp.float32),
                pltpu.SemaphoreType.DMA((2,)),
            ],
        ),
        compiler_params=pltpu.CompilerParams(vmem_limit_bytes=VMEM_BYTES),
        cost_estimate=pl.CostEstimate(
            flops=flops, bytes_accessed=2 * slots * rows * share_src * pieces, transcendentals=0
        ),
    )(scalars, matrix, *sources, incident)


def recent_kernel(slots, parts, cols_count, scalars, matrix, *refs):
    sources = refs[:parts]
    base, kept_out, sent_out, total = refs[parts:]
    part, turn = pl.program_id(0), pl.program_id(1)
    used = scalars[slots]
    share = kept_out.shape[1]

    @pl.when((part == 0) & (turn == 0))
    def _():
        total[...] = jnp.zeros_like(total)

    for which in range(parts):
        @pl.when((part == which) & (turn < used))
        def _():
            total[...] += jnp.dot(matrix[0], sources[which][...], preferred_element_type=jnp.float32)

    @pl.when((part == parts - 1) & (turn == slots - 1))
    def _():
        weight = -scalars[slots + 1].astype(jnp.float32)
        bit = scalars[slots + 2]
        for pair in range(cols_count // 2):
            for out, own in ((kept_out, bit), (sent_out, 1 - bit)):
                rows = pl.ds(pl.multiple_of((2 * pair + own) * share, share), share)
                out[pair] = base[rows, :] + weight * total[rows, :]


def recent_call(scalars, matrix, sources, base, cols_count):
    slots, rows, _ = matrix.shape
    waves = base.shape[1]
    parts = len(sources)
    depth = sources[0].shape[0]
    share = rows // cols_count
    shape = (cols_count // 2, share, waves)
    whole = lambda part, turn, held: (0, 0)
    return pl.pallas_call(
        functools.partial(recent_kernel, slots, parts, cols_count),
        out_shape=[jax.ShapeDtypeStruct(shape, jnp.float32)] * 2,
        grid_spec=pltpu.PrefetchScalarGridSpec(
            num_scalar_prefetch=1,
            grid=(parts, slots),
            in_specs=[
                pl.BlockSpec(
                    (1, rows, depth), lambda part, turn, held: (held[turn], 0, held[slots + 3 + part])
                )
            ]
            + [pl.BlockSpec((depth, waves), whole)] * parts
            + [pl.BlockSpec((rows, waves), whole)],
            out_specs=[pl.BlockSpec(shape, lambda part, turn, held: (0, 0, 0))] * 2,
            scratch_shapes=[pltpu.VMEM((rows, waves), jnp.float32)],
        ),
        compiler_params=pltpu.CompilerParams(vmem_limit_bytes=VMEM_BYTES),
        cost_estimate=pl.CostEstimate(
            flops=2 * slots * rows * depth * parts * waves,
            bytes_accessed=2 * slots * rows * depth * parts,
            transcendentals=0,
        ),
    )(scalars, matrix, *sources, base)


def per_device(rows_count, cols_count, interaction, history, incident, load_gain, load_cubic, delays, tile_map):
    fanout = rows_count // cols_count
    layers = cols_count
    row_index, col_index = lax.axis_index("row"), lax.axis_index("col")
    layer, lane = row_index // fanout, row_index % fanout
    slots, block_obs, _ = interaction.shape
    share = incident.shape[1]
    delay = delays[0, 0]
    weight = tile_map[0, 0]
    bits = [1 << bit for bit in range((cols_count - 1).bit_length())]

    def send(value, target):
        pairs = []
        for row in range(rows_count):
            for col in range(cols_count):
                goal = target(row // fanout, row % fanout, col)
                if goal is not None:
                    pairs.append((row * cols_count + col, (goal[0] * fanout + goal[1]) * cols_count + goal[2]))
        return lax.ppermute(value, BOTH, pairs)

    def along_layers(value):
        return send(value, lambda layer, lane, col: ((layer - 1) % layers, lane, col))

    def along_lanes(value, steps):
        return send(value, lambda layer, lane, col: (layer, (lane - steps) % fanout, col))

    places = jnp.stack(
        [
            (layer + ahead) % layers * fanout + (lane + beside) % fanout
            for ahead in range(layers)
            for beside in range(fanout)
        ]
    )

    def in_row_order(values):
        rows = jnp.arange(rows_count, dtype=jnp.int32)
        held = (rows // fanout - layer) % layers * fanout + (rows % fanout - lane) % fanout
        ordered = jnp.take(jnp.stack(values), held, axis=0)
        return jnp.moveaxis(ordered, 0, 1).reshape(values[0].shape[0], -1, values[0].shape[2])

    if history.shape[1] % 128:
        places = jnp.zeros_like(places)
    past_scalars = jnp.concatenate([delay, jnp.stack([weight, col_index * share]), places]).astype(jnp.int32)
    recent = delay == 1
    order = jnp.argsort(jnp.where(recent, 0, 1), stable=True)
    used = jnp.sum(recent)
    order = order[jnp.minimum(jnp.arange(slots), jnp.maximum(used - 1, 0))]
    lanes_order = jnp.stack([(lane + beside) % fanout for beside in range(fanout)])
    recent_scalars = jnp.concatenate(
        [order, jnp.stack([used, weight, col_index % 2]), lanes_order]
    ).astype(jnp.int32)

    results = []
    for start, stop in split_waves(history.shape[2]):
        moving = history[:, :, start:stop]
        sources = []
        for ahead in range(layers):
            if ahead:
                moving = along_layers(moving)
            sources.append(moving)
            for beside in range(1, fanout):
                sources.append(along_lanes(moving, beside))
        if sources[0].shape[1] % 128:
            sources = [in_row_order(sources)]
        summands, later = past_call(past_scalars, interaction, sources, incident[:, :, start:stop])
        for bit in bits:
            summands = summands + send(
                summands,
                lambda layer, lane, col: (layer, lane, col ^ bit) if (layer ^ col) & (2 * bit - 1) == bit else None,
            )
        current = load_gain[:, None] * summands - load_cubic[:, None] * summands * summands * summands
        current = jnp.where(layer == col_index, current, 0.0).astype(jnp.bfloat16)

        scattered = current.reshape(cols_count, share, stop - start)
        for bit in reversed(bits):
            halves = scattered.reshape(2, bit, share, stop - start)
            own = (col_index // bit) % 2
            moved = send(
                lax.dynamic_index_in_dim(halves, 1 - own, 0, keepdims=False),
                lambda layer, lane, col: (layer, lane, col ^ bit) if (layer ^ col) & (2 * bit - 1) == 0 else None,
            )
            scattered = lax.dynamic_index_in_dim(halves, own, 0, keepdims=False) + moved

        for bit in reversed(bits):
            current = current + send(
                current,
                lambda layer, lane, col: (layer ^ bit, lane, col) if (layer ^ col) & (2 * bit - 1) == 0 else None,
            )
        sources = [current] + [along_lanes(current, beside) for beside in range(1, fanout)]
        kept, sent = recent_call(recent_scalars, interaction, sources, later, cols_count)
        for bit in bits:
            total = kept + send(sent, lambda layer, lane, col: (layer, lane, col ^ bit))
            if 2 * bit < cols_count:
                pairs = total.reshape(total.shape[0] // 2, 2, share, stop - start)
                own = (col_index // (2 * bit)) % 2
                kept = lax.dynamic_index_in_dim(pairs, own, 1, keepdims=False)
                sent = lax.dynamic_index_in_dim(pairs, 1 - own, 1, keepdims=False)
        field = total[0]
        gain = lax.dynamic_slice_in_dim(load_gain, col_index * share, share, 0)[:, None]
        cubic = lax.dynamic_slice_in_dim(load_cubic, col_index * share, share, 0)[:, None]
        last = (gain * field - cubic * field * field * field).astype(jnp.bfloat16)
        results.append(jnp.stack([scattered[0], last]))
    return jnp.concatenate(results, axis=2)


def solution(mesh):
    placed = (
        P(None, "row", "col"),
        P(None, ("col", "row"), None),
        P(None, ("row", "col"), None),
        P("row"),
        P("row"),
        P("row", "col", None),
        P("row", "col"),
    )
    return jax.shard_map(
        functools.partial(per_device, mesh.shape["row"], mesh.shape["col"]),
        mesh=mesh,
        in_specs=placed,
        out_specs=P(None, ("row", "col"), None),
        check_vma=False,
    )
```

time: 371 us -> 266 us (0.72)
  waiting for transfers between devices: 243 us -> 130 us
  starting transfers between devices: 5.76 us -> 65 us
  matrix products: 48.4 us -> 0 us
  Pallas kernels: 0 us -> 45.3 us
  local copies, waits for them, and re-layouts: 38.6 us -> 5.9 us
  between operations: 26.3 us -> 1.66 us
  other arithmetic: 7.85 us -> 13.5 us
    all_gather x2 -> x0, waiting for transfers between devices: 155 us -> none  [the longest x1 119 us: per_device(): past = lax.all_gather(history_currents, 'row', axis=1, tiled=True)]
    ppermute x4 -> x32, waiting for transfers between devices: 29.4 us -> 130 us  [send(): return lax.ppermute(value, BOTH, pairs)]
    ppermute x4 -> x32, starting transfers between devices: 5.63 us -> 65 us  [send(): return lax.ppermute(value, BOTH, pairs)]
    reduce_scatter x2 -> x0, waiting for transfers between devices: 57.9 us -> none  [per_device(): field = lax.psum_scatter(summands, 'col', scatter_dimension=0, tiled=True)]
    dot_general x10 -> x0, matrix products: 48.4 us -> none  [per_device(): jnp.dot(interaction[slot_number], source, preferred_element_type=jnp.floa...]
    pallas_call x0 -> x4, Pallas kernels: none -> 45.3 us  [the longest x2 33.8 us: past_call(): pl.pallas_call(functools.partial(past_kernel, slots, depth, pieces), out_...]
    add x0 -> x12, other arithmetic: none -> 8.06 us  [the longest x4 4.52 us: per_device(): current + send(current, lambda layer, lane, col: (layer ^ bit, lane, col)...]
    concatenate x1 -> x2, local copies, waits for them, and re-layouts: 9.07 us -> 1.44 us  [the longest x1 0.74 us: per_device(): jnp.concatenate([delay, jnp.stack([weight, col_index * share]), places])]
  transfers between devices with their start and end apart: 8 -> 32, of which waited for: 8 -> 19; matrix products, arithmetic and copies ran while one was open for 4% -> 5% of each run, Pallas kernels for 0% -> 17%
where the time goes in v1:
time: 266 us; the launch traced here: 261 us
  waiting for transfers between devices  130 us (49%)
  starting transfers between devices  65 us (24%)
  Pallas kernels  45.3 us (17%)
  other arithmetic  13.5 us (5%)
  local copies, waits for them, and re-layouts  5.9 us (2%)
    ppermute x32, waiting for transfers between devices, send(): return lax.ppermute(value, BOTH, pairs)  130 us
    ppermute x32, starting transfers between devices, send(): return lax.ppermute(value, BOTH, pairs)  65 us
    pallas_call x2, Pallas kernels, past_call(): pl.pallas_call(functools.partial(past_kernel, slots, depth, pieces), out_...  33.8 us
    pallas_call x2, Pallas kernels, recent_call(): pl.pallas_call(functools.partial(recent_kernel, slots, parts, cols_count)...  11.5 us
  transfers between devices with their start and end apart: 32, of which 19 were waited for; matrix products, arithmetic and copies ran while one was open for 5% of the time, Pallas kernels for 17%

profile of v1, /device:TPU:0, one launch (start us, length us, event | category | flops | bytes accessed | tf_op | source)
XLA Modules:
  0.0 261.2 jit_solution(16045431851845767751)
XLA Ops:
  0.0 1.3 fusion.12
  1.3 5.1 %collective-permute-start.17 = (bf16[4,256,256]{2,1,0:T(8,128)(2,1)S(1)}, bf16[4,256,256]{2,1,0:T(8,128)(2,1)S(1)}, u32[]{:S(2)}, u32[]{:S(2)}) collective-permute-start(bf16[4,256,256]{2,1,0:T(8,128)(2,1)S(1)} %get-tuple-element.26.refs_0_), channel_id=1, source_target_pairs={{0,24},{1,25},{2,26},{3,27},{4,28},{5,29},{6,30},{7,31},{8,0},{9,1... | collective-permute-start | bytes 1572872 | tf_op jit(solution)/shard_map/ppermute | solution.py:173
  6.8 11.9 %collective-permute-done.17.refs_2_ = bf16[4,256,256]{2,1,0:T(8,128)(2,1)S(1)} collective-permute-done((bf16[4,256,256]{2,1,0:T(8,128)(2,1)S(1)}, bf16[4,256,256]{2,1,0:T(8,128)(2,1)S(1)}, u32[]{:S(2)}, u32[]{:S(2)}) %collective-permute-start.17) | collective-permute-done | bytes 524320 | tf_op jit(solution)/shard_map/ppermute | solution.py:173
  18.7 4.3 %collective-permute-start.19 = (bf16[4,256,256]{2,1,0:T(8,128)(2,1)S(1)}, bf16[4,256,256]{2,1,0:T(8,128)(2,1)S(1)}, u32[]{:S(2)}, u32[]{:S(2)}) collective-permute-start(bf16[4,256,256]{2,1,0:T(8,128)(2,1)S(1)} %collective-permute-done.17.refs_2_), channel_id=1, source_target_pairs={{0,24},{1,25},{2,26},{3,27},{4,28},{5,29},{6,30},{7,31},{8,0},{9,1... | collective-permute-start | bytes 1572872 | tf_op jit(solution)/shard_map/ppermute | solution.py:173
  23.0 7.0 %collective-permute-done.1.refs_2_ = bf16[4,256,256]{2,1,0:T(8,128)(2,1)S(1)} collective-permute-done((bf16[4,256,256]{2,1,0:T(8,128)(2,1)S(1)}, bf16[4,256,256]{2,1,0:T(8,128)(2,1)S(1)}, u32[]{:S(2)}, u32[]{:S(2)}) %collective-permute-start.1) | collective-permute-done | bytes 524320 | tf_op jit(solution)/shard_map/ppermute | solution.py:173
  29.9 4.3 %collective-permute-start.3 = (bf16[4,256,256]{2,1,0:T(8,128)(2,1)S(1)}, bf16[4,256,256]{2,1,0:T(8,128)(2,1)S(1)}, u32[]{:S(2)}, u32[]{:S(2)}) collective-permute-start(bf16[4,256,256]{2,1,0:T(8,128)(2,1)S(1)} %collective-permute-done.1.refs_2_), channel_id=1, source_target_pairs={{0,24},{1,25},{2,26},{3,27},{4,28},{5,29},{6,30},{7,31},{8,0},{9,1... | collective-permute-start | bytes 1572872 | tf_op jit(solution)/shard_map/ppermute | solution.py:173
  34.2 7.0 %collective-permute-done.19.refs_4_ = bf16[4,256,256]{2,1,0:T(8,128)(2,1)S(1)} collective-permute-done((bf16[4,256,256]{2,1,0:T(8,128)(2,1)S(1)}, bf16[4,256,256]{2,1,0:T(8,128)(2,1)S(1)}, u32[]{:S(2)}, u32[]{:S(2)}) %collective-permute-start.19) | collective-permute-done | bytes 524320 | tf_op jit(solution)/shard_map/ppermute | solution.py:173
  41.2 4.3 %collective-permute-start.21 = (bf16[4,256,256]{2,1,0:T(8,128)(2,1)S(1)}, bf16[4,256,256]{2,1,0:T(8,128)(2,1)}, u32[]{:S(2)}, u32[]{:S(2)}) collective-permute-start(bf16[4,256,256]{2,1,0:T(8,128)(2,1)S(1)} %collective-permute-done.19.refs_4_), channel_id=1, source_target_pairs={{0,24},{1,25},{2,26},{3,27},{4,28},{5,29},{6,30},{7,31},{8,0},{9,1... | collective-permute-start | bytes 1572872 | tf_op jit(solution)/shard_map/ppermute | solution.py:173
  45.5 1.5 collective-permute-start.16
  47.5 1.5 collective-permute-start.20
  49.0 3.4 %collective-permute-done.3.refs_4_ = bf16[4,256,256]{2,1,0:T(8,128)(2,1)S(1)} collective-permute-done((bf16[4,256,256]{2,1,0:T(8,128)(2,1)S(1)}, bf16[4,256,256]{2,1,0:T(8,128)(2,1)S(1)}, u32[]{:S(2)}, u32[]{:S(2)}) %collective-permute-start.3) | collective-permute-done | bytes 524320 | tf_op jit(solution)/shard_map/ppermute | solution.py:173
  52.4 4.3 %collective-permute-start.5 = (bf16[4,256,256]{2,1,0:T(8,128)(2,1)S(1)}, bf16[4,256,256]{2,1,0:T(8,128)(2,1)}, u32[]{:S(2)}, u32[]{:S(2)}) collective-permute-start(bf16[4,256,256]{2,1,0:T(8,128)(2,1)S(1)} %collective-permute-done.3.refs_4_), channel_id=1, source_target_pairs={{0,24},{1,25},{2,26},{3,27},{4,28},{5,29},{6,30},{7,31},{8,0},{9,1... | collective-permute-start | bytes 1572872 | tf_op jit(solution)/shard_map/ppermute | solution.py:173
  56.7 7.0 %collective-permute-done.21.refs_6_ = bf16[4,256,256]{2,1,0:T(8,128)(2,1)} collective-permute-done((bf16[4,256,256]{2,1,0:T(8,128)(2,1)S(1)}, bf16[4,256,256]{2,1,0:T(8,128)(2,1)}, u32[]{:S(2)}, u32[]{:S(2)}) %collective-permute-start.21) | collective-permute-done | bytes 524320 | tf_op jit(solution)/shard_map/ppermute | solution.py:173
  63.6 1.5 collective-permute-start.22
  65.8 0.7 concatenate.9.scalars
  66.5 1.3 fusion.11
  68.4 3.2 %collective-permute-done.18.refs_3_ = bf16[4,256,256]{2,1,0:T(8,128)(2,1)} collective-permute-done((bf16[4,256,256]{2,1,0:T(8,128)(2,1)S(1)}, bf16[4,256,256]{2,1,0:T(8,128)(2,1)}, u32[]{:S(2)}, u32[]{:S(2)}) %collective-permute-start.18) | collective-permute-done | bytes 524320 | tf_op jit(solution)/shard_map/ppermute | solution.py:173
  71.7 1.5 collective-permute-start.2
  73.1 9.7 %collective-permute-done.20.refs_5_ = bf16[4,256,256]{2,1,0:T(8,128)(2,1)} collective-permute-done((bf16[4,256,256]{2,1,0:T(8,128)(2,1)S(1)}, bf16[4,256,256]{2,1,0:T(8,128)(2,1)}, u32[]{:S(2)}, u32[]{:S(2)}) %collective-permute-start.20) | collective-permute-done | bytes 524320 | tf_op jit(solution)/shard_map/ppermute | solution.py:173
  82.9 1.5 collective-permute-start.4
  84.9 9.2 %collective-permute-done.22.refs_7_ = bf16[4,256,256]{2,1,0:T(8,128)(2,1)} collective-permute-done((bf16[4,256,256]{2,1,0:T(8,128)(2,1)}, bf16[4,256,256]{2,1,0:T(8,128)(2,1)}, u32[]{:S(2)}, u32[]{:S(2)}) %collective-permute-start.22) | collective-permute-done | bytes 524320 | tf_op jit(solution)/shard_map/ppermute | solution.py:173
  94.1 16.9 %shard_map.75 = (f32[1024,256]{1,0:T(8,128)S(1)}, f32[1024,256]{1,0:T(8,128)}) custom-call(s32[15]{0:T(128)S(1)} %concatenate.9.scalars, bf16[5,1024,2048]{2,1,0:T(8,128)(2,1)} %matrix.7, bf16[4,256,256]{2,1,0:T(8,128)(2,1)S(1)} %get-tuple-element.26.refs_0_, bf16[4,256,256]{2,1,0:T(8,128)(2,1)} %collective-permute-done.16.refs_1_, ...), custom_call_target="tpu_custom_call" | custom-call | flops 10737418240 | bytes 20971520 | tf_op jit(solution)/shard_map/pallas_call | solution.py:73
  111.1 1.3 collective-permute-start.23
  112.4 4.1 %collective-permute-done.2.refs_3_ = bf16[4,256,256]{2,1,0:T(8,128)(2,1)S(1)} collective-permute-done((bf16[4,256,256]{2,1,0:T(8,128)(2,1)S(1)}, bf16[4,256,256]{2,1,0:T(8,128)(2,1)S(1)}, u32[]{:S(2)}, u32[]{:S(2)}) %collective-permute-start.2) | collective-permute-done | bytes 524320 | tf_op jit(solution)/shard_map/ppermute | solution.py:173
  116.5 11.2 %collective-permute-done.4.refs_5_ = bf16[4,256,256]{2,1,0:T(8,128)(2,1)S(1)} collective-permute-done((bf16[4,256,256]{2,1,0:T(8,128)(2,1)S(1)}, bf16[4,256,256]{2,1,0:T(8,128)(2,1)S(1)}, u32[]{:S(2)}, u32[]{:S(2)}) %collective-permute-start.4) | collective-permute-done | bytes 524320 | tf_op jit(solution)/shard_map/ppermute | solution.py:173
  127.7 7.7 %collective-permute-done.6.refs_7_ = bf16[4,256,256]{2,1,0:T(8,128)(2,1)S(1)} collective-permute-done((bf16[4,256,256]{2,1,0:T(8,128)(2,1)}, bf16[4,256,256]{2,1,0:T(8,128)(2,1)S(1)}, u32[]{:S(2)}, u32[]{:S(2)}) %collective-permute-start.6) | collective-permute-done | bytes 524320 | tf_op jit(solution)/shard_map/ppermute | solution.py:173
  135.5 16.9 %shard_map.73 = (f32[1024,256]{1,0:T(8,128)S(1)}, f32[1024,256]{1,0:T(8,128)}) custom-call(s32[15]{0:T(128)S(1)} %concatenate.9.scalars, bf16[5,1024,2048]{2,1,0:T(8,128)(2,1)} %matrix.7, bf16[4,256,256]{2,1,0:T(8,128)(2,1)S(1)} %get-tuple-element.25.refs_0_, bf16[4,256,256]{2,1,0:T(8,128)(2,1)S(1)} %collective-permute-done.refs_1_, ...), custom_call_target="tpu_custom_call" | custom-call | flops 10737418240 | bytes 20971520 | tf_op jit(solution)/shard_map/pallas_call | solution.py:73
  152.4 1.4 collective-permute-start.7
  153.8 1.2 add.206
  155.0 1.3 collective-permute-start.24
  156.3 0.8 collective-permute-done.7
  157.1 1.1 add.191
  158.2 1.3 collective-permute-start.8
  159.5 12.5 %collective-permute-done.24 = f32[1024,256]{1,0:T(8,128)} collective-permute-done((f32[1024,256]{1,0:T(8,128)}, f32[1024,256]{1,0:T(8,128)}, u32[]{:S(2)}, u32[]{:S(2)}) %collective-permute-start.24) | collective-permute-done | bytes 1048608 | tf_op jit(solution)/shard_map/ppermute | solution.py:173
  172.0 11.2 %collective-permute-done.8 = f32[1024,256]{1,0:T(8,128)} collective-permute-done((f32[1024,256]{1,0:T(8,128)}, f32[1024,256]{1,0:T(8,128)}, u32[]{:S(2)}, u32[]{:S(2)}) %collective-permute-start.8) | collective-permute-done | bytes 1048608 | tf_op jit(solution)/shard_map/ppermute | solution.py:173
  183.2 2.7 %fusion.2 = (bf16[1024,256]{1,0:T(8,128)(2,1)S(1)}, bf16[1024,256]{1,0:T(8,128)(2,1)S(1)}) fusion(f32[1024,256]{1,0:T(8,128)} %add.191, f32[1024,256]{1,0:T(8,128)} %collective-permute-done.8, f32[1024]{0:T(1024)S(1)} %copy-done.6, f32[1024]{0:T(1024)S(1)} %copy-done.5, pred[]{:T(512)S(6)} %eq.34, f32[1024,256]{1,0:T(8,128)} %add.206, ...), kind=kLoop, calls=%fused_computation.5 | loop fusion | flops 4194304 | bytes 5251073 | tf_op jit(solution)/shard_map/convert_element_type | solution.py:226
  186.0 1.3 collective-permute-start.27
  187.3 1.3 collective-permute-start.11
  188.7 5.4 %collective-permute-done.27 = bf16[1024,256]{1,0:T(8,128)(2,1)S(1)} collective-permute-done((bf16[1024,256]{1,0:T(8,128)(2,1)S(1)}, bf16[1024,256]{1,0:T(8,128)(2,1)S(1)}, u32[]{:S(2)}, u32[]{:S(2)}) %collective-permute-start.27) | collective-permute-done | bytes 524320 | tf_op jit(solution)/shard_map/ppermute | solution.py:173
  194.0 0.9 add.210
  195.0 2.1 collective-permute-start.28
  197.1 2.6 collective-permute-done.11
  199.6 0.9 add.202
  200.6 2.1 collective-permute-start.12
  202.7 0.6 fusion.10
  204.0 11.3 %collective-permute-start.9 = (bf16[2,256,256]{2,1,0:T(8,128)(2,1)S(1)}, bf16[2,256,256]{2,1,0:T(8,128)(2,1)}, u32[]{:S(2)}, u32[]{:S(2)}) collective-permute-start(bf16[2,256,256]{2,1,0:T(8,128)(2,1)S(1)} %dynamic-slice_bitcast_fusion.1), channel_id=1, source_target_pairs={{0,2},{4,6},{9,11},{13,15},{18,16},{22,20},{27,25},{31,29}} | collective-permute-start | bytes 786440 | tf_op jit(solution)/shard_map/ppermute | solution.py:173
  215.2 1.3 add.211.refs_0_
  216.6 1.5 collective-permute-start.29
  218.2 1.0 sort.17
  219.2 0.6 gather_fusion
  219.9 0.7 concatenate.10.scalars
  220.6 1.0 dynamic-slice_bitcast_fusion
  221.6 1.3 collective-permute-start.25
  222.9 1.3 add.203.refs_0_
  224.9 1.1 bitcast_add_fusion.1
  225.9 4.7 %collective-permute-done.29.refs_1_ = bf16[1024,256]{1,0:T(8,128)(2,1)S(1)} collective-permute-done((bf16[1024,256]{1,0:T(8,128)(2,1)S(1)}, bf16[1024,256]{1,0:T(8,128)(2,1)S(1)}, u32[]{:S(2)}, u32[]{:S(2)}) %collective-permute-start.29) | collective-permute-done | bytes 524320 | tf_op jit(solution)/shard_map/ppermute | solution.py:173
  230.6 5.7 %shard_map.76 = (f32[2,256,256]{2,1,0:T(8,128)S(1)}, f32[2,256,256]{2,1,0:T(8,128)S(1)}) custom-call(s32[10]{0:T(128)S(1)} %concatenate.10.scalars, bf16[5,1024,2048]{2,1,0:T(8,128)(2,1)} %matrix.7, bf16[1024,256]{1,0:T(8,128)(2,1)S(1)} %add.211.refs_0_, bf16[1024,256]{1,0:T(8,128)(2,1)S(1)} %collective-permute-done.29.refs_1_, f32[1024,256]{1,0:T(8,128)S(1)} %copy-done), custom_call_target="tpu_custom_call" | custom-call | flops 5368709120 | bytes 20971520 | tf_op jit(solution)/shard_map/pallas_call | solution.py:130
  236.5 5.7 %shard_map.74 = (f32[2,256,256]{2,1,0:T(8,128)S(1)}, f32[2,256,256]{2,1,0:T(8,128)S(1)}) custom-call(s32[10]{0:T(128)S(1)} %concatenate.10.scalars, bf16[5,1024,2048]{2,1,0:T(8,128)(2,1)} %matrix.7, bf16[1024,256]{1,0:T(8,128)(2,1)S(1)} %add.203.refs_0_, bf16[1024,256]{1,0:T(8,128)(2,1)S(1)} %collective-permute-done.13.refs_1_, f32[1024,256]{1,0:T(8,128)S(1)} %copy-done.1), custom_call_target="tpu_custom_call" | custom-call | flops 5368709120 | bytes 20971520 | tf_op jit(solution)/shard_map/pallas_call | solution.py:130
  242.3 2.4 collective-permute-start.10
  244.8 1.3 collective-permute-start.26
  246.2 2.5 collective-permute-start.31
  249.0 6.9 %collective-permute-done.31 = f32[1,256,256]{2,1,0:T(8,128)S(1)} collective-permute-done((f32[1,256,256]{2,1,0:T(8,128)S(1)}, f32[1,256,256]{2,1,0:T(8,128)S(1)}, u32[]{:S(2)}, u32[]{:S(2)}) %collective-permute-start.31) | collective-permute-done | bytes 262176 | tf_op jit(solution)/shard_map/ppermute | solution.py:173
  255.9 4.3 %collective-permute-done.15 = f32[1,256,256]{2,1,0:T(8,128)S(1)} collective-permute-done((f32[1,256,256]{2,1,0:T(8,128)S(1)}, f32[1,256,256]{2,1,0:T(8,128)S(1)}, u32[]{:S(2)}, u32[]{:S(2)}) %collective-permute-start.15) | collective-permute-done | bytes 262176 | tf_op jit(solution)/shard_map/ppermute | solution.py:173
  260.4 0.8 maximum_maximum_fusion
  (53 shorter events, 3.7 us)
Async XLA Ops:
  1.3 17.4 %collective-permute-start.17 = (bf16[4,256,256]{2,1,0:T(8,128)(2,1)S(1)}, bf16[4,256,256]{2,1,0:T(8,128)(2,1)S(1)}, u32[]{:S(2)}, u32[]{:S(2)}) collective-permute-start(bf16[4,256,256]{2,1,0:T(8,128)(2,1)S(1)} %get-tuple-element.26.refs_0_), channel_id=1, source_target_pairs={{0,24},{1,25},{2,26},{3,27},{4,28},{5,29},{6,30},{7,31},{8,0},{9,1... | collective-permute-start | bytes 1572872 | tf_op jit(solution)/shard_map/ppermute | solution.py:173
  6.4 23.6 %collective-permute-start.1 = (bf16[4,256,256]{2,1,0:T(8,128)(2,1)S(1)}, bf16[4,256,256]{2,1,0:T(8,128)(2,1)S(1)}, u32[]{:S(2)}, u32[]{:S(2)}) collective-permute-start(bf16[4,256,256]{2,1,0:T(8,128)(2,1)S(1)} %get-tuple-element.25.refs_0_), channel_id=1, source_target_pairs={{0,24},{1,25},{2,26},{3,27},{4,28},{5,29},{6,30},{7,31},{8,0},{9,1... | collective-permute-start | bytes 1572872 | tf_op jit(solution)/shard_map/ppermute | solution.py:173
  18.7 22.5 %collective-permute-start.19 = (bf16[4,256,256]{2,1,0:T(8,128)(2,1)S(1)}, bf16[4,256,256]{2,1,0:T(8,128)(2,1)S(1)}, u32[]{:S(2)}, u32[]{:S(2)}) collective-permute-start(bf16[4,256,256]{2,1,0:T(8,128)(2,1)S(1)} %collective-permute-done.17.refs_2_), channel_id=1, source_target_pairs={{0,24},{1,25},{2,26},{3,27},{4,28},{5,29},{6,30},{7,31},{8,0},{9,1... | collective-permute-start | bytes 1572872 | tf_op jit(solution)/shard_map/ppermute | solution.py:173
  29.9 22.5 %collective-permute-start.3 = (bf16[4,256,256]{2,1,0:T(8,128)(2,1)S(1)}, bf16[4,256,256]{2,1,0:T(8,128)(2,1)S(1)}, u32[]{:S(2)}, u32[]{:S(2)}) collective-permute-start(bf16[4,256,256]{2,1,0:T(8,128)(2,1)S(1)} %collective-permute-done.1.refs_2_), channel_id=1, source_target_pairs={{0,24},{1,25},{2,26},{3,27},{4,28},{5,29},{6,30},{7,31},{8,0},{9,1... | collective-permute-start | bytes 1572872 | tf_op jit(solution)/shard_map/ppermute | solution.py:173
  41.2 22.5 %collective-permute-start.21 = (bf16[4,256,256]{2,1,0:T(8,128)(2,1)S(1)}, bf16[4,256,256]{2,1,0:T(8,128)(2,1)}, u32[]{:S(2)}, u32[]{:S(2)}) collective-permute-start(bf16[4,256,256]{2,1,0:T(8,128)(2,1)S(1)} %collective-permute-done.19.refs_4_), channel_id=1, source_target_pairs={{0,24},{1,25},{2,26},{3,27},{4,28},{5,29},{6,30},{7,31},{8,0},{9,1... | collective-permute-start | bytes 1572872 | tf_op jit(solution)/shard_map/ppermute | solution.py:173
  45.5 22.4 %collective-permute-start.16 = (bf16[4,256,256]{2,1,0:T(8,128)(2,1)S(1)}, bf16[4,256,256]{2,1,0:T(8,128)(2,1)}, u32[]{:S(2)}, u32[]{:S(2)}) collective-permute-start(bf16[4,256,256]{2,1,0:T(8,128)(2,1)S(1)} %get-tuple-element.26.refs_0_), channel_id=1, source_target_pairs={{0,4},{1,5},{2,6},{3,7},{4,0},{5,1},{6,2},{7,3},{8,12},{9,13},{10,... | collective-permute-start | bytes 1572872 | tf_op jit(solution)/shard_map/ppermute | solution.py:173
  46.9 24.7 %collective-permute-start.18 = (bf16[4,256,256]{2,1,0:T(8,128)(2,1)S(1)}, bf16[4,256,256]{2,1,0:T(8,128)(2,1)}, u32[]{:S(2)}, u32[]{:S(2)}) collective-permute-start(bf16[4,256,256]{2,1,0:T(8,128)(2,1)S(1)} %collective-permute-done.17.refs_2_), channel_id=1, source_target_pairs={{0,4},{1,5},{2,6},{3,7},{4,0},{5,1},{6,2},{7,3},{8,12},{9,13},{10,... | collective-permute-start | bytes 1572872 | tf_op jit(solution)/shard_map/ppermute | solution.py:173
  47.5 35.4 %collective-permute-start.20 = (bf16[4,256,256]{2,1,0:T(8,128)(2,1)S(1)}, bf16[4,256,256]{2,1,0:T(8,128)(2,1)}, u32[]{:S(2)}, u32[]{:S(2)}) collective-permute-start(bf16[4,256,256]{2,1,0:T(8,128)(2,1)S(1)} %collective-permute-done.19.refs_4_), channel_id=1, source_target_pairs={{0,4},{1,5},{2,6},{3,7},{4,0},{5,1},{6,2},{7,3},{8,12},{9,13},{10,... | collective-permute-start | bytes 1572872 | tf_op jit(solution)/shard_map/ppermute | solution.py:173
  52.4 32.0 %collective-permute-start.5 = (bf16[4,256,256]{2,1,0:T(8,128)(2,1)S(1)}, bf16[4,256,256]{2,1,0:T(8,128)(2,1)}, u32[]{:S(2)}, u32[]{:S(2)}) collective-permute-start(bf16[4,256,256]{2,1,0:T(8,128)(2,1)S(1)} %collective-permute-done.3.refs_4_), channel_id=1, source_target_pairs={{0,24},{1,25},{2,26},{3,27},{4,28},{5,29},{6,30},{7,31},{8,0},{9,1... | collective-permute-start | bytes 1572872 | tf_op jit(solution)/shard_map/ppermute | solution.py:173
  63.6 30.5 %collective-permute-start.22 = (bf16[4,256,256]{2,1,0:T(8,128)(2,1)}, bf16[4,256,256]{2,1,0:T(8,128)(2,1)}, u32[]{:S(2)}, u32[]{:S(2)}) collective-permute-start(bf16[4,256,256]{2,1,0:T(8,128)(2,1)} %collective-permute-done.21.refs_6_), channel_id=1, source_target_pairs={{0,4},{1,5},{2,6},{3,7},{4,0},{5,1},{6,2},{7,3},{8,12},{9,13},{10,... | collective-permute-start | bytes 1572872 | tf_op jit(solution)/shard_map/ppermute | solution.py:173
  67.8 44.5 %collective-permute-start = (bf16[4,256,256]{2,1,0:T(8,128)(2,1)S(1)}, bf16[4,256,256]{2,1,0:T(8,128)(2,1)S(1)}, u32[]{:S(2)}, u32[]{:S(2)}) collective-permute-start(bf16[4,256,256]{2,1,0:T(8,128)(2,1)S(1)} %get-tuple-element.25.refs_0_), channel_id=1, source_target_pairs={{0,4},{1,5},{2,6},{3,7},{4,0},{5,1},{6,2},{7,3},{8,12},{9,13},{10,... | collective-permute-start | bytes 1572872 | tf_op jit(solution)/shard_map/ppermute | solution.py:173
  71.7 44.8 %collective-permute-start.2 = (bf16[4,256,256]{2,1,0:T(8,128)(2,1)S(1)}, bf16[4,256,256]{2,1,0:T(8,128)(2,1)S(1)}, u32[]{:S(2)}, u32[]{:S(2)}) collective-permute-start(bf16[4,256,256]{2,1,0:T(8,128)(2,1)S(1)} %collective-permute-done.1.refs_2_), channel_id=1, source_target_pairs={{0,4},{1,5},{2,6},{3,7},{4,0},{5,1},{6,2},{7,3},{8,12},{9,13},{10,... | collective-permute-start | bytes 1572872 | tf_op jit(solution)/shard_map/ppermute | solution.py:173
  82.9 44.8 %collective-permute-start.4 = (bf16[4,256,256]{2,1,0:T(8,128)(2,1)S(1)}, bf16[4,256,256]{2,1,0:T(8,128)(2,1)S(1)}, u32[]{:S(2)}, u32[]{:S(2)}) collective-permute-start(bf16[4,256,256]{2,1,0:T(8,128)(2,1)S(1)} %collective-permute-done.3.refs_4_), channel_id=1, source_target_pairs={{0,4},{1,5},{2,6},{3,7},{4,0},{5,1},{6,2},{7,3},{8,12},{9,13},{10,... | collective-permute-start | bytes 1572872 | tf_op jit(solution)/shard_map/ppermute | solution.py:173
  84.4 51.1 %collective-permute-start.6 = (bf16[4,256,256]{2,1,0:T(8,128)(2,1)}, bf16[4,256,256]{2,1,0:T(8,128)(2,1)S(1)}, u32[]{:S(2)}, u32[]{:S(2)}) collective-permute-start(bf16[4,256,256]{2,1,0:T(8,128)(2,1)} %collective-permute-done.5.refs_6_), channel_id=1, source_target_pairs={{0,4},{1,5},{2,6},{3,7},{4,0},{5,1},{6,2},{7,3},{8,12},{9,13},{10,... | collective-permute-start | bytes 1572872 | tf_op jit(solution)/shard_map/ppermute | solution.py:173
  111.1 42.8 %collective-permute-start.23 = (f32[1024,256]{1,0:T(8,128)S(1)}, f32[1024,256]{1,0:T(8,128)S(1)}, u32[]{:S(2)}, u32[]{:S(2)}) collective-permute-start(f32[1024,256]{1,0:T(8,128)S(1)} %get-tuple-element.19), channel_id=1, source_target_pairs={{1,0},{3,2},{5,4},{7,6},{8,9},{10,11},{12,13},{14,15},{17,16},{19,... | collective-permute-start | bytes 3145736 | tf_op jit(solution)/shard_map/ppermute | solution.py:173
  135.5 47.8 %copy-start.5 = (f32[1024]{0:T(1024)S(1)}, f32[1024]{0:T(1024)}, u32[]{:S(2)}) copy-start(f32[1024]{0:T(1024)} %param.10) | copy-start | bytes 12292
  135.5 47.8 %copy-start.6 = (f32[1024]{0:T(1024)S(1)}, f32[1024]{0:T(1024)}, u32[]{:S(2)}) copy-start(f32[1024]{0:T(1024)} %param.11) | copy-start | bytes 12292
  135.5 67.2 %copy-start.7 = (s32[1,1,5]{2,1,0:T(1,128)S(1)}, s32[1,1,5]{2,1,0:T(1,128)}, u32[]{:S(2)}) copy-start(s32[1,1,5]{2,1,0:T(1,128)} %param.12) | copy-start | bytes 64
  135.5 95.2 %copy-start = (f32[1024,256]{1,0:T(8,128)S(1)}, f32[1024,256]{1,0:T(8,128)}, u32[]{:S(2)}) copy-start(f32[1024,256]{1,0:T(8,128)} %get-tuple-element.20.refs_2_) | copy-start | bytes 3145732
  152.4 84.1 %copy-start.1 = (f32[1024,256]{1,0:T(8,128)S(1)}, f32[1024,256]{1,0:T(8,128)}, u32[]{:S(2)}) copy-start(f32[1024,256]{1,0:T(8,128)} %get-tuple-element.16.refs_2_) | copy-start | bytes 3145732
  152.4 4.7 %collective-permute-start.7 = (f32[1024,256]{1,0:T(8,128)S(1)}, f32[1024,256]{1,0:T(8,128)S(1)}, u32[]{:S(2)}, u32[]{:S(2)}) collective-permute-start(f32[1024,256]{1,0:T(8,128)S(1)} %get-tuple-element.14), channel_id=1, source_target_pairs={{1,0},{3,2},{5,4},{7,6},{8,9},{10,11},{12,13},{14,15},{17,16},{19,... | collective-permute-start | bytes 3145736 | tf_op jit(solution)/shard_map/ppermute | solution.py:173
  155.0 17.0 %collective-permute-start.24 = (f32[1024,256]{1,0:T(8,128)}, f32[1024,256]{1,0:T(8,128)}, u32[]{:S(2)}, u32[]{:S(2)}) collective-permute-start(f32[1024,256]{1,0:T(8,128)} %add.206), channel_id=1, source_target_pairs={{2,0},{6,4},{11,9},{15,13},{16,18},{20,22},{25,27},{29,31}} | collective-permute-start | bytes 3145736 | tf_op jit(solution)/shard_map/ppermute | solution.py:173
  158.2 25.0 %collective-permute-start.8 = (f32[1024,256]{1,0:T(8,128)}, f32[1024,256]{1,0:T(8,128)}, u32[]{:S(2)}, u32[]{:S(2)}) collective-permute-start(f32[1024,256]{1,0:T(8,128)} %add.191), channel_id=1, source_target_pairs={{2,0},{6,4},{11,9},{15,13},{16,18},{20,22},{25,27},{29,31}} | collective-permute-start | bytes 3145736 | tf_op jit(solution)/shard_map/ppermute | solution.py:173
  186.0 29.2 %copy-start.2 = (bf16[1024,256]{1,0:T(8,128)(2,1)}, bf16[1024,256]{1,0:T(8,128)(2,1)S(1)}, u32[]{:S(2)}) copy-start(bf16[1024,256]{1,0:T(8,128)(2,1)S(1)} %get-tuple-element.28) | copy-start | bytes 1572868
  186.0 29.2 %copy-start.4 = (bf16[1024,256]{1,0:T(8,128)(2,1)}, bf16[1024,256]{1,0:T(8,128)(2,1)S(1)}, u32[]{:S(2)}) copy-start(bf16[1024,256]{1,0:T(8,128)(2,1)S(1)} %get-tuple-element.27) | copy-start | bytes 1572868
  186.0 8.0 %collective-permute-start.27 = (bf16[1024,256]{1,0:T(8,128)(2,1)S(1)}, bf16[1024,256]{1,0:T(8,128)(2,1)S(1)}, u32[]{:S(2)}, u32[]{:S(2)}) collective-permute-start(bf16[1024,256]{1,0:T(8,128)(2,1)S(1)} %get-tuple-element.28), channel_id=1, source_target_pairs={{0,16},{4,20},{9,25},{13,29},{18,2},{22,6},{27,11},{31,15}} | collective-permute-start | bytes 1572872 | tf_op jit(solution)/shard_map/ppermute | solution.py:173
  187.3 12.3 %collective-permute-start.11 = (bf16[1024,256]{1,0:T(8,128)(2,1)S(1)}, bf16[1024,256]{1,0:T(8,128)(2,1)S(1)}, u32[]{:S(2)}, u32[]{:S(2)}) collective-permute-start(bf16[1024,256]{1,0:T(8,128)(2,1)S(1)} %get-tuple-element.27), channel_id=1, source_target_pairs={{0,16},{4,20},{9,25},{13,29},{18,2},{22,6},{27,11},{31,15}} | collective-permute-start | bytes 1572872 | tf_op jit(solution)/shard_map/ppermute | solution.py:173
  195.0 20.3 %collective-permute-start.28 = (bf16[1024,256]{1,0:T(8,128)(2,1)}, bf16[1024,256]{1,0:T(8,128)(2,1)}, u32[]{:S(2)}, u32[]{:S(2)}) collective-permute-start(bf16[1024,256]{1,0:T(8,128)(2,1)} %add.210), channel_id=1, source_target_pairs={{0,8},{2,10},{4,12},{6,14},{9,1},{11,3},{13,5},{15,7},{16,24},{18,... | collective-permute-start | bytes 1572872 | tf_op jit(solution)/shard_map/ppermute | solution.py:173
  200.6 22.3 %collective-permute-start.12 = (bf16[1024,256]{1,0:T(8,128)(2,1)}, bf16[1024,256]{1,0:T(8,128)(2,1)}, u32[]{:S(2)}, u32[]{:S(2)}) collective-permute-start(bf16[1024,256]{1,0:T(8,128)(2,1)} %add.202), channel_id=1, source_target_pairs={{0,8},{2,10},{4,12},{6,14},{9,1},{11,3},{13,5},{15,7},{16,24},{18,... | collective-permute-start | bytes 1572872 | tf_op jit(solution)/shard_map/ppermute | solution.py:173
  204.0 20.9 %collective-permute-start.9 = (bf16[2,256,256]{2,1,0:T(8,128)(2,1)S(1)}, bf16[2,256,256]{2,1,0:T(8,128)(2,1)}, u32[]{:S(2)}, u32[]{:S(2)}) collective-permute-start(bf16[2,256,256]{2,1,0:T(8,128)(2,1)S(1)} %dynamic-slice_bitcast_fusion.1), channel_id=1, source_target_pairs={{0,2},{4,6},{9,11},{13,15},{18,16},{22,20},{27,25},{31,29}} | collective-permute-start | bytes 786440 | tf_op jit(solution)/shard_map/ppermute | solution.py:173
  216.6 14.1 %collective-permute-start.29 = (bf16[1024,256]{1,0:T(8,128)(2,1)S(1)}, bf16[1024,256]{1,0:T(8,128)(2,1)S(1)}, u32[]{:S(2)}, u32[]{:S(2)}) collective-permute-start(bf16[1024,256]{1,0:T(8,128)(2,1)S(1)} %add.211.refs_0_), channel_id=1, source_target_pairs={{0,4},{1,5},{2,6},{3,7},{4,0},{5,1},{6,2},{7,3},{8,12},{9,13},{10,... | collective-permute-start | bytes 1572872 | tf_op jit(solution)/shard_map/ppermute | solution.py:173
  221.6 23.2 %collective-permute-start.25 = (bf16[2,256,256]{2,1,0:T(8,128)(2,1)S(1)}, bf16[2,256,256]{2,1,0:T(8,128)(2,1)S(1)}, u32[]{:S(2)}, u32[]{:S(2)}) collective-permute-start(bf16[2,256,256]{2,1,0:T(8,128)(2,1)S(1)} %dynamic-slice_bitcast_fusion), channel_id=1, source_target_pairs={{0,2},{4,6},{9,11},{13,15},{18,16},{22,20},{27,25},{31,29}} | collective-permute-start | bytes 786440 | tf_op jit(solution)/shard_map/ppermute | solution.py:173
  224.2 12.2 %collective-permute-start.13 = (bf16[1024,256]{1,0:T(8,128)(2,1)S(1)}, bf16[1024,256]{1,0:T(8,128)(2,1)S(1)}, u32[]{:S(2)}, u32[]{:S(2)}) collective-permute-start(bf16[1024,256]{1,0:T(8,128)(2,1)S(1)} %add.203.refs_0_), channel_id=1, source_target_pairs={{0,4},{1,5},{2,6},{3,7},{4,0},{5,1},{6,2},{7,3},{8,12},{9,13},{10,... | collective-permute-start | bytes 1572872 | tf_op jit(solution)/shard_map/ppermute | solution.py:173
  230.6 14.1 %copy-start.3 = (bf16[1024,256]{1,0:T(8,128)(2,1)S(1)}, bf16[1024,256]{1,0:T(8,128)(2,1)}, u32[]{:S(2)}) copy-start(bf16[1024,256]{1,0:T(8,128)(2,1)} %copy-done.2) | copy-start | bytes 1572868
  236.4 9.7 %collective-permute-start.30 = (f32[2,256,256]{2,1,0:T(8,128)S(1)}, f32[2,256,256]{2,1,0:T(8,128)S(1)}, u32[]{:S(2)}, u32[]{:S(2)}) collective-permute-start(f32[2,256,256]{2,1,0:T(8,128)S(1)} %get-tuple-element.22), channel_id=1, source_target_pairs={{0,1},{1,0},{2,3},{3,2},{4,5},{5,4},{6,7},{7,6},{8,9},{9,8},{10,11... | collective-permute-start | bytes 1572872 | tf_op jit(solution)/shard_map/ppermute | solution.py:173
  242.2 6.5 %collective-permute-start.14 = (f32[2,256,256]{2,1,0:T(8,128)S(1)}, f32[2,256,256]{2,1,0:T(8,128)S(1)}, u32[]{:S(2)}, u32[]{:S(2)}) collective-permute-start(f32[2,256,256]{2,1,0:T(8,128)S(1)} %get-tuple-element.18), channel_id=1, source_target_pairs={{0,1},{1,0},{2,3},{3,2},{4,5},{5,4},{6,7},{7,6},{8,9},{9,8},{10,11... | collective-permute-start | bytes 1572872 | tf_op jit(solution)/shard_map/ppermute | solution.py:173
  242.3 6.6 %collective-permute-start.10 = (bf16[1,256,256]{2,1,0:T(8,128)(2,1)S(1)}, bf16[1,256,256]{2,1,0:T(8,128)(2,1)S(1)}, u32[]{:S(2)}, u32[]{:S(2)}) collective-permute-start(bf16[1,256,256]{2,1,0:T(8,128)(2,1)S(1)} %constant_dynamic-slice_fusion.3), channel_id=1, source_target_pairs={{0,1},{2,3},{4,5},{6,7},{9,8},{11,10},{13,12},{15,14},{16,17},{18,... | collective-permute-start | bytes 393224 | tf_op jit(solution)/shard_map/ppermute | solution.py:173
  244.8 4.2 %collective-permute-start.26 = (bf16[1,256,256]{2,1,0:T(8,128)(2,1)S(1)}, bf16[1,256,256]{2,1,0:T(8,128)(2,1)S(1)}, u32[]{:S(2)}, u32[]{:S(2)}) collective-permute-start(bf16[1,256,256]{2,1,0:T(8,128)(2,1)S(1)} %constant_dynamic-slice_fusion.1), channel_id=1, source_target_pairs={{0,1},{2,3},{4,5},{6,7},{9,8},{11,10},{13,12},{15,14},{16,17},{18,... | collective-permute-start | bytes 393224 | tf_op jit(solution)/shard_map/ppermute | solution.py:173
  246.2 9.7 %collective-permute-start.31 = (f32[1,256,256]{2,1,0:T(8,128)S(1)}, f32[1,256,256]{2,1,0:T(8,128)S(1)}, u32[]{:S(2)}, u32[]{:S(2)}) collective-permute-start(f32[1,256,256]{2,1,0:T(8,128)S(1)} %constant_dynamic-slice_fusion), channel_id=1, source_target_pairs={{0,2},{1,3},{2,0},{3,1},{4,6},{5,7},{6,4},{7,5},{8,10},{9,11},{10,... | collective-permute-start | bytes 786440 | tf_op jit(solution)/shard_map/ppermute | solution.py:173
  248.8 11.4 %collective-permute-start.15 = (f32[1,256,256]{2,1,0:T(8,128)S(1)}, f32[1,256,256]{2,1,0:T(8,128)S(1)}, u32[]{:S(2)}, u32[]{:S(2)}) collective-permute-start(f32[1,256,256]{2,1,0:T(8,128)S(1)} %constant_dynamic-slice_fusion.2), channel_id=1, source_target_pairs={{0,2},{1,3},{2,0},{3,1},{4,6},{5,7},{6,4},{7,5},{8,10},{9,11},{10,... | collective-permute-start | bytes 786440 | tf_op jit(solution)/shard_map/ppermute | solution.py:173

commit v2 on v0

v2 whole, which is shorter than its diff:
```python
import functools

import jax
import jax.numpy as jnp
from jax import lax
from jax.experimental import pallas as pl
from jax.experimental.pallas import tpu as pltpu
from jax.sharding import PartitionSpec as P

BOTH = ("row", "col")
VMEM_BYTES = 8 * 1024 * 1024
TILE = 16
LANES = 128
LEVELS = 32000.0
IN_VMEM = pl.BlockSpec(memory_space=pltpu.VMEM)
IN_SMEM = pl.BlockSpec(memory_space=pltpu.SMEM)


def split_waves(waves):
    unit = 128
    if waves % unit or waves < 2 * unit:
        return [(0, waves)]
    half = (waves // unit + 1) // 2 * unit
    return [(0, half), (half, waves)]


def whereabouts(fanout):
    row = lax.axis_index("row")
    return lax.div(row, fanout), lax.rem(row, fanout), lax.axis_index("col")


def cycle_row(layers, fanout, place):
    lane, along = lax.div(place, layers), lax.rem(place, layers)
    return jnp.where(lax.rem(lane, 2) == 0, along, layers - 1 - along) * fanout + lane


def cycle_place(layers, layer, lane):
    return lane * layers + jnp.where(lax.rem(lane, 2) == 0, layer, layers - 1 - layer)


def first_kernel(matrix, gain, cubic, mark, own_gain, own_cubic, held):
    mark[...] = matrix[0, :8, :128].astype(jnp.float32)
    share = own_gain.shape[0]
    own = pl.ds(pl.multiple_of(lax.axis_index("col") * share, share), share)
    for source, out in ((gain, own_gain), (cubic, own_cubic)):
        for number in range(source.shape[0]):
            line = jnp.broadcast_to(source[number : number + 1, :], (LANES, LANES))
            held[number * LANES : (number + 1) * LANES, :] = jnp.transpose(line)
        out[...] = held[own, :]


def first_call(matrix, gain, cubic, share):
    rows = matrix.shape[1]
    lines = (rows // LANES, LANES)
    return pl.pallas_call(
        first_kernel,
        out_shape=[jax.ShapeDtypeStruct((8, LANES), jnp.float32)]
        + [jax.ShapeDtypeStruct((share, LANES), jnp.float32)] * 2,
        in_specs=[IN_VMEM] * 3,
        out_specs=[IN_VMEM] * 3,
        scratch_shapes=[pltpu.VMEM((rows, LANES), jnp.float32)],
        compiler_params=pltpu.CompilerParams(vmem_limit_bytes=VMEM_BYTES),
        cost_estimate=pl.CostEstimate(flops=0, bytes_accessed=4096, transcendentals=0),
    )(matrix, gain.reshape(lines), cubic.reshape(lines))


def past_kernel(number, opening, closing, layers, fanout, delays, tile, matrix, front, back, mark, *refs):
    refs = list(refs)
    carried = None if opening else refs.pop(0)
    incident = refs.pop(0) if closing else None
    slots = matrix.shape[0]
    depth, half, waves = front.shape
    layer, lane, col = whereabouts(fanout)
    count = matrix.shape[2] // (2 * half)
    here = cycle_place(layers, layer, lane)
    left, right = [], []
    for side, piece in enumerate((front, back)):
        if count == 1:
            place = side
        else:
            walked = lax.rem(here + (number if side else count - number), count)
            place = 2 * cycle_row(layers, fanout, walked) + side
        columns = pl.ds(pl.multiple_of(place * half, half), half)
        for slot in range(slots):
            delay = delays[slot]
            now = piece[depth - delay]
            later = piece[jnp.minimum(depth + 1 - delay, depth - 1)]
            later = jnp.where(delay >= 2, later, jnp.zeros_like(later))
            right.append(jnp.concatenate([now, later], axis=1))
            left.append(matrix[slot, :, columns])
    left, right = jnp.concatenate(left, axis=1), jnp.concatenate(right, axis=0)
    total = jnp.dot(left, right, preferred_element_type=jnp.float32)
    if not opening:
        total = total + carried[...]
    if not closing:
        refs[0][...] = total
        refs[1][...] = jnp.zeros_like(refs[1])
        return
    kept, sent, later, held = refs
    held[...] = -tile[0].astype(jnp.float32) * total
    share = incident.shape[1]
    own = pl.ds(pl.multiple_of(col * share, share), share)
    later[...] = held[:, waves:]
    later[own, :] += incident[1]
    bit = lax.rem(col, 2)
    for pair in range(kept.shape[0]):
        for out, which in ((kept, bit), (sent, 1 - bit)):
            rows = pl.ds(pl.multiple_of((2 * pair + which) * share, share), share)
            out[pair] = held[rows, :waves]
    kept[lax.div(col, 2)] += incident[0]


def past_call(delays, tile, matrix, pieces, mark, carried, incident, number, layers, fanout):
    slots, rows, _ = matrix.shape
    _, half, waves = pieces[0].shape
    totals = jax.ShapeDtypeStruct((rows, 2 * waves), jnp.float32)
    operands = [delays, tile, matrix, *pieces, mark]
    aliases, scratch = {}, []
    if carried is not None:
        operands.append(carried)
    if incident is None:
        ends = [totals, jax.ShapeDtypeStruct((8, 128), jnp.float32)]
        aliases = {} if carried is None else {6: 0}
    else:
        operands.append(incident)
        share = incident.shape[1]
        ends = [jax.ShapeDtypeStruct((rows // share // 2, share, waves), jnp.float32)] * 2
        ends.append(jax.ShapeDtypeStruct((rows, waves), jnp.float32))
        scratch = [pltpu.VMEM(totals.shape, jnp.float32)]
    return pl.pallas_call(
        functools.partial(past_kernel, number, carried is None, incident is not None, layers, fanout),
        out_shape=ends,
        in_specs=[IN_SMEM] * 2 + [IN_VMEM] * (len(operands) - 2),
        out_specs=[IN_VMEM] * len(ends),
        scratch_shapes=scratch,
        input_output_aliases=aliases,
        compiler_params=pltpu.CompilerParams(vmem_limit_bytes=VMEM_BYTES),
        cost_estimate=pl.CostEstimate(
            flops=8 * slots * rows * half * waves, bytes_accessed=4 * slots * rows * half, transcendentals=0
        ),
    )(*operands)


def small_call(kernel, shapes, matrix, *operands):
    return pl.pallas_call(
        kernel,
        out_shape=shapes,
        in_specs=[IN_VMEM] * (1 + len(operands)),
        out_specs=[IN_VMEM] * len(shapes),
        compiler_params=pltpu.CompilerParams(vmem_limit_bytes=VMEM_BYTES),
        cost_estimate=pl.CostEstimate(flops=0, bytes_accessed=1 << 20, transcendentals=0),
    )(matrix, *operands)


def fold_kernel(bit, last, matrix, kept, got, kept_out, sent_out):
    own = lax.rem(lax.div(lax.axis_index("col"), bit), 2)
    for pair in range(kept_out.shape[0]):
        kept_out[pair] = kept[2 * pair + own] + got[2 * pair + own]
        sent = kept[2 * pair + 1 - own] + got[2 * pair + 1 - own]
        if not last:
            sent_out[pair] = sent
            continue
        rows = sent.shape[0]
        peak = jnp.maximum(jnp.max(jnp.abs(sent), axis=0, keepdims=True), 1e-30)
        power = jnp.ceil(jnp.log2(peak))
        coded = jnp.round(sent * (jnp.exp2(-power) * LEVELS))
        sent_out[:rows] = coded.astype(jnp.int32).astype(jnp.int16)
        sent_out[rows:] = jnp.broadcast_to(power, (TILE, sent.shape[1])).astype(jnp.int32).astype(jnp.int16)


def fold_call(matrix, kept, got, bit, last):
    pairs, (share, waves) = kept.shape[0] // 2, kept.shape[1:]
    shapes = [jax.ShapeDtypeStruct((pairs, share, waves), jnp.float32)]
    if last:
        shapes.append(jax.ShapeDtypeStruct((share + TILE, waves), jnp.int16))
    else:
        shapes.append(shapes[0])
    return small_call(functools.partial(fold_kernel, bit, last), shapes, matrix, kept, got)


def load_kernel(matrix, kept, got, gain, cubic, out):
    share, waves = out.shape
    gain, cubic = (jnp.concatenate([ref[...]] * (waves // LANES), axis=1) for ref in (gain, cubic))
    power = got[share:].astype(jnp.int32).astype(jnp.float32)[:1]
    field = kept[0] + got[:share].astype(jnp.int32).astype(jnp.float32) * (jnp.exp2(power) * (1.0 / LEVELS))
    out[...] = (gain * field - cubic * field * field * field).astype(jnp.bfloat16)


def load_call(matrix, kept, got, gain, cubic):
    shapes = [jax.ShapeDtypeStruct(kept.shape[1:], jnp.bfloat16)]
    return small_call(load_kernel, shapes, matrix, kept, got, gain, cubic)[0]


def arrange_kernel(layers, fanout, matrix, *refs):
    layer, _, col = whereabouts(fanout)
    apart = layer ^ col
    for place in range(layers):
        @pl.when(apart == place)
        def _():
            for other in range(layers):
                refs[layers + other][...] = refs[place ^ other][...]


def arrange_call(matrix, values, fanout):
    shapes = [jax.ShapeDtypeStruct(value.shape, value.dtype) for value in values]
    return small_call(functools.partial(arrange_kernel, len(values), fanout), shapes, matrix, *values)


def recent_kernel(fanout, cols_count, delays, tile, matrix, *refs):
    sources = refs[: fanout * cols_count]
    base, kept, sent, held, total = refs[fanout * cols_count :]
    slots = matrix.shape[0]
    share = sources[0].shape[0]
    _, lane, col = whereabouts(fanout)
    for beside in range(fanout):
        for other in range(cols_count):
            place = lax.rem(lane + beside, fanout) * cols_count + (col ^ other)
            held[pl.ds(pl.multiple_of(place * share, share), share), :] = sources[beside * cols_count + other][...]
    total[...] = jnp.zeros_like(total)
    for slot in range(slots):
        @pl.when(delays[slot] == 1)
        def _():
            total[...] += jnp.dot(matrix[slot], held[...], preferred_element_type=jnp.float32)

    weight = -tile[0].astype(jnp.float32)
    bit = lax.rem(col, 2)
    for pair in range(cols_count // 2):
        for out, own in ((kept, bit), (sent, 1 - bit)):
            rows = pl.ds(pl.multiple_of((2 * pair + own) * share, share), share)
            out[pair] = base[rows, :] + weight * total[rows, :]


def recent_call(delays, tile, matrix, sources, base, fanout, cols_count):
    slots, rows, depth = matrix.shape
    share, waves = sources[0].shape
    return pl.pallas_call(
        functools.partial(recent_kernel, fanout, cols_count),
        out_shape=[jax.ShapeDtypeStruct((rows // share // 2, share, waves), jnp.float32)] * 2,
        in_specs=[IN_SMEM] * 2 + [IN_VMEM] * (len(sources) + 2),
        out_specs=[IN_VMEM] * 2,
        scratch_shapes=[pltpu.VMEM((depth, waves), jnp.bfloat16), pltpu.VMEM((rows, waves), jnp.float32)],
        compiler_params=pltpu.CompilerParams(vmem_limit_bytes=VMEM_BYTES),
        cost_estimate=pl.CostEstimate(
            flops=2 * slots * rows * depth * waves, bytes_accessed=2 * slots * rows * depth, transcendentals=0
        ),
    )(delays, tile, matrix, *sources, base)


def per_device(rows_count, cols_count, interaction, history, incident, load_gain, load_cubic, delays, tile_map):
    fanout = rows_count // cols_count
    layers = cols_count
    share = incident.shape[1]
    delay, tile = delays.reshape(-1), tile_map.reshape(-1)
    bits = [1 << bit for bit in range((cols_count - 1).bit_length())]

    def send(value, target):
        pairs = []
        for row in range(rows_count):
            for col in range(cols_count):
                goal = target(row // fanout, row % fanout, col)
                if goal is not None:
                    pairs.append((row * cols_count + col, (goal[0] * fanout + goal[1]) * cols_count + goal[2]))
        return lax.ppermute(value, BOTH, pairs)

    cycle = [
        (layer if lane % 2 == 0 else layers - 1 - layer) * fanout + lane
        for lane in range(fanout)
        for layer in range(layers)
    ]
    spot = {row: place for place, row in enumerate(cycle)}

    def around(value, steps):
        pairs = [(row, cycle[(spot[row] + steps) % rows_count]) for row in range(rows_count)]
        return lax.ppermute(value, "row", pairs)

    aligned = history.shape[1] % 256 == 0

    def in_row_order(values, sense):
        row = lax.axis_index("row")
        here = jnp.asarray([spot[row] for row in range(rows_count)], jnp.int32)[row]
        rows = jnp.asarray(cycle, jnp.int32)[(here - sense * jnp.arange(rows_count)) % rows_count]
        return jnp.take(jnp.stack(values), jnp.argsort(rows), axis=0)

    mark, gain, cubic = first_call(interaction, load_gain, load_cubic, share)

    def summed_and_loaded(kept, sent):
        for bit in bits:
            got = send(sent, lambda layer, lane, col: (layer, lane, col ^ bit))
            if bit != bits[-1]:
                kept, sent = fold_call(interaction, kept, got, 2 * bit, 2 * bit == bits[-1])
        return load_call(interaction, kept, got, gain, cubic)

    def to_layers(current, earlier):
        by_layer = {0: current}
        for bit in bits:
            for apart in list(by_layer):
                if apart == 0 and bit == 1 and earlier is not None:
                    by_layer[0], earlier[1] = lax.optimization_barrier((by_layer[0], earlier[1]))
                by_layer[apart ^ bit] = send(by_layer[apart], lambda layer, lane, col: (layer ^ bit, lane, col))
        return by_layer

    def to_sources(by_layer):
        ordered = arrange_call(interaction, [by_layer[apart] for apart in range(layers)], fanout)
        sources = {}
        for beside in reversed(range(fanout)):
            for other in range(cols_count):
                value = ordered[other]
                if beside or other:
                    value = send(
                        value, lambda layer, lane, col: (layer, (lane - beside) % fanout, col ^ other)
                    )
                sources[beside, other] = value
        return [sources[beside, other] for beside in range(fanout) for other in range(cols_count)]

    chunks = split_waves(history.shape[2])
    half = history.shape[1] // 2
    moving = [(history[:, :half, start:stop], history[:, half:, start:stop]) for start, stop in chunks]
    carried, marks = [None] * len(chunks), [None] * len(chunks)
    arrived = [[moving[number]] for number in range(len(chunks))]

    def add_piece(number, step):
        start, stop = chunks[number]
        ending = incident[:, :, start:stop] if step == rows_count - 1 else None
        outs = past_call(
            delay,
            tile,
            interaction,
            arrived[number][step],
            marks[number],
            carried[number],
            ending,
            step,
            layers,
            fanout,
        )
        carried[number], marks[number] = (outs[0], outs[1]) if ending is None else (outs, None)

    marks = [mark] * len(chunks)
    added = [0] * len(chunks)
    for step in range(1, rows_count):
        for number in range(len(chunks)):
            front, back = arrived[number][-1]
            if step >= 2 and aligned:
                wanted = 0 if step == 2 else 1 if step == 3 else step - 1
                while added[number] < wanted:
                    add_piece(number, added[number])
                    added[number] += 1
                front, back, marks[number] = lax.optimization_barrier((front, back, marks[number]))
            arrived[number].append((around(front, 1), around(back, -1)))
    if aligned:
        for step in range(rows_count):
            for number in range(len(chunks)):
                if step >= added[number]:
                    add_piece(number, step)
    if not aligned:
        for number, (start, stop) in enumerate(chunks):
            fronts, backs = zip(*arrived[number])
            ordered = jnp.stack([in_row_order(fronts, 1), in_row_order(backs, -1)], axis=1)
            ordered = jnp.moveaxis(ordered, 2, 0).reshape(history.shape[0], 2, rows_count * half, stop - start)
            pieces = ordered[:, 0], ordered[:, 1]
            ending = incident[:, :, start:stop]
            carried[number] = past_call(
                delay, tile, interaction, pieces, marks[number], None, ending, 0, layers, fanout
            )
    by_layers, results = [], []
    for kept, sent, _ in carried:
        current = summed_and_loaded(kept, sent)
        by_layers.append(to_layers(current, by_layers[-1] if by_layers else None))
    for by_layer, (_, _, later) in zip(by_layers, carried):
        kept, sent = recent_call(delay, tile, interaction, to_sources(by_layer), later, fanout, cols_count)
        results.append(jnp.stack([by_layer[0], summed_and_loaded(kept, sent)]))
    return jnp.concatenate(results, axis=2)


def solution(mesh):
    placed = (
        P(None, "row", "col"),
        P(None, ("col", "row"), None),
        P(None, ("row", "col"), None),
        P("row"),
        P("row"),
        P("row", "col", None),
        P("row", "col"),
    )
    return jax.shard_map(
        functools.partial(per_device, mesh.shape["row"], mesh.shape["col"]),
        mesh=mesh,
        in_specs=placed,
        out_specs=P(None, ("row", "col"), None),
        check_vma=False,
    )
```

time: 371 us -> 164 us (0.44)
  waiting for transfers between devices: 243 us -> 54.9 us
  starting transfers between devices: 5.76 us -> 59 us
  matrix products: 48.4 us -> 0 us
  Pallas kernels: 0 us -> 40.4 us
  local copies, waits for them, and re-layouts: 38.6 us -> 8.35 us
  between operations: 26.3 us -> 1.1 us
  other arithmetic: 7.85 us -> 0.83 us
    all_gather x2 -> x0, waiting for transfers between devices: 155 us -> none  [the longest x1 119 us: per_device(): past = lax.all_gather(history_currents, 'row', axis=1, tiled=True)]
    reduce_scatter x2 -> x0, waiting for transfers between devices: 57.9 us -> none  [per_device(): field = lax.psum_scatter(summands, 'col', scatter_dimension=0, tiled=True)]
    ppermute x4 -> x56, starting transfers between devices: 5.63 us -> 59 us  [the longest x28 29.6 us: around(): return lax.ppermute(value, 'row', pairs)]
    dot_general x10 -> x0, matrix products: 48.4 us -> none  [per_device(): jnp.dot(interaction[slot_number], source, preferred_element_type=jnp.floa...]
    pallas_call x0 -> x29, Pallas kernels: none -> 40.4 us  [the longest x16 34.7 us: past_call(): pl.pallas_call(functools.partial(past_kernel, number, carried is None, in...]
    ppermute x4 -> x56, waiting for transfers between devices: 29.4 us -> 54.9 us  [the longest x28 39.5 us: send(): return lax.ppermute(value, BOTH, pairs)]
    concatenate x1 -> x0, local copies, waits for them, and re-layouts: 9.07 us -> none  [per_device(): jnp.concatenate([past, jnp.zeros((STEPS,) + past.shape[1:], jnp.bfloat16)...]
    gather x1 -> x0, local copies, waits for them, and re-layouts: 7.8 us -> none  [route_share(): picked = jnp.take(grid, order, axis=0)]
  transfers between devices with their start and end apart: 8 -> 56, of which waited for: 8 -> 27; matrix products, arithmetic and copies ran while one was open for 4% -> 0% of each run, Pallas kernels for 0% -> 24%
where the time goes in v2:
time: 164 us; the launch traced here: 165 us
  starting transfers between devices  59 us (36%)
  waiting for transfers between devices  54.9 us (33%)
  Pallas kernels  40.4 us (25%)
  local copies, waits for them, and re-layouts  8.35 us (5%)
    ppermute x28, waiting for transfers between devices, send(): return lax.ppermute(value, BOTH, pairs)  39.5 us
    pallas_call x16, Pallas kernels, past_call(): pl.pallas_call(functools.partial(past_kernel, number, carried is None, in...  34.7 us
    ppermute x28, starting transfers between devices, around(): return lax.ppermute(value, 'row', pairs)  29.6 us
    ppermute x28, starting transfers between devices, send(): return lax.ppermute(value, BOTH, pairs)  29.4 us
    ppermute x28, waiting for transfers between devices, around(): return lax.ppermute(value, 'row', pairs)  15.4 us
    unnamed x12, local copies, waits for them, and re-layouts  6.98 us
    pallas_call x2, Pallas kernels, recent_call(): pl.pallas_call(functools.partial(recent_kernel, fanout, cols_count), out_...  4.47 us
  transfers between devices with their start and end apart: 56, of which 27 were waited for; matrix products, arithmetic and copies ran while one was open for 0% of the time, Pallas kernels for 24%

profile of v2, /device:TPU:0, one launch (start us, length us, event | category | flops | bytes accessed | tf_op | source)
XLA Modules:
  0.0 164.7 jit_solution(17634252700477472318)
XLA Ops:
  1.3 3.1 %collective-permute-start = (bf16[4,128,256]{2,1,0:T(8,128)(2,1)S(1)}, bf16[4,128,256]{2,1,0:T(8,128)(2,1)S(1)}, u32[]{:S(2)}, u32[]{:S(2)}) collective-permute-start(bf16[4,128,256]{2,1,0:T(8,128)(2,1)S(1)} %get-tuple-element.198.front), channel_id=1, source_target_pairs={{0,8},{4,0},{8,16},{12,4},{16,24},{20,12},{24,28},{28,20},{1,9},{5... | collective-permute-start | bytes 786440 | tf_op jit(solution)/shard_map/ppermute | solution.py:274
  4.4 2.0 %collective-permute-start.16 = (bf16[4,128,256]{2,1,0:T(8,128)(2,1)S(1)}, bf16[4,128,256]{2,1,0:T(8,128)(2,1)S(1)}, u32[]{:S(2)}, u32[]{:S(2)}) collective-permute-start(bf16[4,128,256]{2,1,0:T(8,128)(2,1)S(1)} %get-tuple-element.200.front), channel_id=1, source_target_pairs={{0,8},{4,0},{8,16},{12,4},{16,24},{20,12},{24,28},{28,20},{1,9},{5... | collective-permute-start | bytes 786440 | tf_op jit(solution)/shard_map/ppermute | solution.py:274
  6.4 7.0 %copy-done = bf16[5,1024,2048]{2,1,0:T(8,128)(2,1)S(1)} copy-done((bf16[5,1024,2048]{2,1,0:T(8,128)(2,1)S(1)}, bf16[5,1024,2048]{2,1,0:T(8,128)(2,1)}, u32[]{:S(2)}) %copy-start) | copy-done | bytes 20971544
  13.8 2.1 %collective-permute-start.2 = (bf16[4,128,256]{2,1,0:T(8,128)(2,1)S(1)}, bf16[4,128,256]{2,1,0:T(8,128)(2,1)S(1)}, u32[]{:S(2)}, u32[]{:S(2)}) collective-permute-start(bf16[4,128,256]{2,1,0:T(8,128)(2,1)S(1)} %collective-permute-done.front), channel_id=1, source_target_pairs={{0,8},{4,0},{8,16},{12,4},{16,24},{20,12},{24,28},{28,20},{1,9},{5... | collective-permute-start | bytes 786440 | tf_op jit(solution)/shard_map/ppermute | solution.py:274
  16.9 1.6 collective-permute-done.17.back
  18.6 1.6 collective-permute-start.18
  21.3 2.1 %shard_map.74 = (f32[1024,512]{1,0:T(8,128)S(1)}, f32[8,128]{1,0:T(8,128)S(1)}) custom-call(s32[5]{0:T(128)S(1)} %bitcast.30, s32[1]{0:T(128)} %bitcast.8.tile, bf16[5,1024,2048]{2,1,0:T(8,128)(2,1)S(1)} %copy-done.1, bf16[4,128,256]{2,1,0:T(8,128)(2,1)S(1)} %get-tuple-element.198.front, bf16[4,128,256]{2,1,0:T(8,128)(2,1)S(1)} %get-tuple-element.197.back, ...), custom_call_target="tpu_custom_call" | custom-call | flops 1342177280 | bytes 2621440 | tf_op jit(solution)/shard_map/pallas_call | solution.py:130
  23.4 1.7 %collective-permute-done.3.back = bf16[4,128,256]{2,1,0:T(8,128)(2,1)S(1)} collective-permute-done((bf16[4,128,256]{2,1,0:T(8,128)(2,1)S(1)}, bf16[4,128,256]{2,1,0:T(8,128)(2,1)S(1)}, u32[]{:S(2)}, u32[]{:S(2)}) %collective-permute-start.3) | collective-permute-done | bytes 262176 | tf_op jit(solution)/shard_map/ppermute | solution.py:274
  25.1 1.6 collective-permute-start.4
  27.1 2.1 %shard_map.84 = (f32[1024,512]{1,0:T(8,128)S(1)}, f32[8,128]{1,0:T(8,128)S(1)}) custom-call(s32[5]{0:T(128)S(1)} %bitcast.31, s32[1]{0:T(128)} %bitcast.16.tile, bf16[5,1024,2048]{2,1,0:T(8,128)(2,1)S(1)} %copy-done.1, bf16[4,128,256]{2,1,0:T(8,128)(2,1)S(1)} %get-tuple-element.200.front, bf16[4,128,256]{2,1,0:T(8,128)(2,1)S(1)} %get-tuple-element.199.back, ...), custom_call_target="tpu_custom_call" | custom-call | flops 1342177280 | bytes 2621440 | tf_op jit(solution)/shard_map/pallas_call | solution.py:130
  29.2 1.5 collective-permute-done.19.back
  30.7 1.6 collective-permute-start.20
  32.8 2.1 %shard_map.75 = (f32[1024,512]{1,0:T(8,128)S(1)}, f32[8,128]{1,0:T(8,128)S(1)}) custom-call(s32[5]{0:T(128)S(1)} %bitcast.32, s32[1]{0:T(128)} %bitcast.9.tile, bf16[5,1024,2048]{2,1,0:T(8,128)(2,1)S(1)} %copy-done.1, bf16[4,128,256]{2,1,0:T(8,128)(2,1)S(1)} %collective-permute-done.front, ...), custom_call_target="tpu_custom_call", output_to_operand_aliasing={{0}: (6, {})} | custom-call | flops 1342177280 | bytes 2621440 | tf_op jit(solution)/shard_map/pallas_call | solution.py:130
  34.9 2.1 %shard_map.76 = (f32[1024,512]{1,0:T(8,128)S(1)}, f32[8,128]{1,0:T(8,128)S(1)}) custom-call(s32[5]{0:T(128)S(1)} %bitcast.33, s32[1]{0:T(128)} %bitcast.10.tile, bf16[5,1024,2048]{2,1,0:T(8,128)(2,1)S(1)} %copy-done.1, bf16[4,128,256]{2,1,0:T(8,128)(2,1)S(1)} %collective-permute-done.2.front, ...), custom_call_target="tpu_custom_call", output_to_operand_aliasing={{0}: (6, {})} | custom-call | flops 1342177280 | bytes 2621440 | tf_op jit(solution)/shard_map/pallas_call | solution.py:130
  37.1 1.6 collective-permute-start.6
  39.2 2.1 %shard_map.85 = (f32[1024,512]{1,0:T(8,128)S(1)}, f32[8,128]{1,0:T(8,128)S(1)}) custom-call(s32[5]{0:T(128)S(1)} %bitcast.34, s32[1]{0:T(128)} %bitcast.17.tile, bf16[5,1024,2048]{2,1,0:T(8,128)(2,1)S(1)} %copy-done.1, bf16[4,128,256]{2,1,0:T(8,128)(2,1)S(1)} %collective-permute-done.16.front, ...), custom_call_target="tpu_custom_call", output_to_operand_aliasing={{0}: (6, {})} | custom-call | flops 1342177280 | bytes 2621440 | tf_op jit(solution)/shard_map/pallas_call | solution.py:130
  41.3 2.1 %shard_map.86 = (f32[1024,512]{1,0:T(8,128)S(1)}, f32[8,128]{1,0:T(8,128)S(1)}) custom-call(s32[5]{0:T(128)S(1)} %bitcast.35, s32[1]{0:T(128)} %bitcast.18.tile, bf16[5,1024,2048]{2,1,0:T(8,128)(2,1)S(1)} %copy-done.1, bf16[4,128,256]{2,1,0:T(8,128)(2,1)S(1)} %collective-permute-done.18.front, ...), custom_call_target="tpu_custom_call", output_to_operand_aliasing={{0}: (6, {})} | custom-call | flops 1342177280 | bytes 2621440 | tf_op jit(solution)/shard_map/pallas_call | solution.py:130
  43.5 1.6 collective-permute-start.22
  45.6 2.1 %shard_map.77 = (f32[1024,512]{1,0:T(8,128)S(1)}, f32[8,128]{1,0:T(8,128)S(1)}) custom-call(s32[5]{0:T(128)S(1)} %bitcast.36, s32[1]{0:T(128)} %bitcast.11.tile, bf16[5,1024,2048]{2,1,0:T(8,128)(2,1)S(1)} %copy-done.1, bf16[4,128,256]{2,1,0:T(8,128)(2,1)S(1)} %collective-permute-done.4.front, ...), custom_call_target="tpu_custom_call", output_to_operand_aliasing={{0}: (6, {})} | custom-call | flops 1342177280 | bytes 2621440 | tf_op jit(solution)/shard_map/pallas_call | solution.py:130
  47.9 1.6 collective-permute-start.8
  50.0 2.1 %shard_map.87 = (f32[1024,512]{1,0:T(8,128)S(1)}, f32[8,128]{1,0:T(8,128)S(1)}) custom-call(s32[5]{0:T(128)S(1)} %bitcast.37, s32[1]{0:T(128)} %bitcast.19.tile, bf16[5,1024,2048]{2,1,0:T(8,128)(2,1)S(1)} %copy-done.1, bf16[4,128,256]{2,1,0:T(8,128)(2,1)S(1)} %collective-permute-done.20.front, ...), custom_call_target="tpu_custom_call", output_to_operand_aliasing={{0}: (6, {})} | custom-call | flops 1342177280 | bytes 2621440 | tf_op jit(solution)/shard_map/pallas_call | solution.py:130
  52.8 1.6 collective-permute-done.23.back
  54.3 1.6 collective-permute-start.24
  56.4 2.1 %shard_map.78 = (f32[1024,512]{1,0:T(8,128)S(1)}, f32[8,128]{1,0:T(8,128)S(1)}) custom-call(s32[5]{0:T(128)S(1)} %bitcast.38, s32[1]{0:T(128)} %bitcast.12.tile, bf16[5,1024,2048]{2,1,0:T(8,128)(2,1)S(1)} %copy-done.1, bf16[4,128,256]{2,1,0:T(8,128)(2,1)S(1)} %collective-permute-done.6.front, ...), custom_call_target="tpu_custom_call", output_to_operand_aliasing={{0}: (6, {})} | custom-call | flops 1342177280 | bytes 2621440 | tf_op jit(solution)/shard_map/pallas_call | solution.py:130
  58.5 1.4 collective-permute-done.9.back
  60.0 1.6 collective-permute-start.10
  62.0 2.1 %shard_map.88 = (f32[1024,512]{1,0:T(8,128)S(1)}, f32[8,128]{1,0:T(8,128)S(1)}) custom-call(s32[5]{0:T(128)S(1)} %bitcast.39, s32[1]{0:T(128)} %bitcast.20.tile, bf16[5,1024,2048]{2,1,0:T(8,128)(2,1)S(1)} %copy-done.1, bf16[4,128,256]{2,1,0:T(8,128)(2,1)S(1)} %collective-permute-done.22.front, ...), custom_call_target="tpu_custom_call", output_to_operand_aliasing={{0}: (6, {})} | custom-call | flops 1342177280 | bytes 2621440 | tf_op jit(solution)/shard_map/pallas_call | solution.py:130
  64.1 1.4 collective-permute-done.25.back
  65.6 1.6 collective-permute-start.26
  67.6 2.1 %shard_map.79 = (f32[1024,512]{1,0:T(8,128)S(1)}, f32[8,128]{1,0:T(8,128)S(1)}) custom-call(s32[5]{0:T(128)S(1)} %bitcast.40, s32[1]{0:T(128)} %bitcast.13.tile, bf16[5,1024,2048]{2,1,0:T(8,128)(2,1)S(1)} %copy-done.1, bf16[4,128,256]{2,1,0:T(8,128)(2,1)S(1)} %collective-permute-done.8.front, ...), custom_call_target="tpu_custom_call", output_to_operand_aliasing={{0}: (6, {})} | custom-call | flops 1342177280 | bytes 2621440 | tf_op jit(solution)/shard_map/pallas_call | solution.py:130
  69.8 1.4 collective-permute-done.11.back
  71.2 1.6 collective-permute-start.12
  73.3 2.1 %shard_map.89 = (f32[1024,512]{1,0:T(8,128)S(1)}, f32[8,128]{1,0:T(8,128)S(1)}) custom-call(s32[5]{0:T(128)S(1)} %bitcast.41, s32[1]{0:T(128)} %bitcast.21.tile, bf16[5,1024,2048]{2,1,0:T(8,128)(2,1)S(1)} %copy-done.1, bf16[4,128,256]{2,1,0:T(8,128)(2,1)S(1)} %collective-permute-done.24.front, ...), custom_call_target="tpu_custom_call", output_to_operand_aliasing={{0}: (6, {})} | custom-call | flops 1342177280 | bytes 2621440 | tf_op jit(solution)/shard_map/pallas_call | solution.py:130
  76.8 1.6 collective-permute-start.28
  78.8 2.1 %shard_map.80 = (f32[1024,512]{1,0:T(8,128)S(1)}, f32[8,128]{1,0:T(8,128)S(1)}) custom-call(s32[5]{0:T(128)S(1)} %bitcast.42, s32[1]{0:T(128)} %bitcast.14.tile, bf16[5,1024,2048]{2,1,0:T(8,128)(2,1)S(1)} %copy-done.1, bf16[4,128,256]{2,1,0:T(8,128)(2,1)S(1)} %collective-permute-done.10.front, ...), custom_call_target="tpu_custom_call", output_to_operand_aliasing={{0}: (6, {})} | custom-call | flops 1342177280 | bytes 2621440 | tf_op jit(solution)/shard_map/pallas_call | solution.py:130
  82.4 2.4 %shard_map.81 = (f32[2,256,256]{2,1,0:T(8,128)S(1)}, f32[2,256,256]{2,1,0:T(8,128)S(1)}, f32[1024,256]{1,0:T(8,128)S(1)}) custom-call(s32[5]{0:T(128)S(1)} %bitcast.43, s32[1]{0:T(128)} %bitcast.15.tile, bf16[5,1024,2048]{2,1,0:T(8,128)(2,1)S(1)} %copy-done.1, bf16[4,128,256]{2,1,0:T(8,128)(2,1)S(1)} %collective-permute-done.12.front, ...), custom_call_target="tpu_custom_call" | custom-call | flops 1342177280 | bytes 2621440 | tf_op jit(solution)/shard_map/pallas_call | solution.py:130
  84.9 2.1 %shard_map.90 = (f32[1024,512]{1,0:T(8,128)S(1)}, f32[8,128]{1,0:T(8,128)S(1)}) custom-call(s32[5]{0:T(128)S(1)} %bitcast.44, s32[1]{0:T(128)} %bitcast.22.tile, bf16[5,1024,2048]{2,1,0:T(8,128)(2,1)S(1)} %copy-done.1, bf16[4,128,256]{2,1,0:T(8,128)(2,1)S(1)} %collective-permute-done.26.front, ...), custom_call_target="tpu_custom_call", output_to_operand_aliasing={{0}: (6, {})} | custom-call | flops 1342177280 | bytes 2621440 | tf_op jit(solution)/shard_map/pallas_call | solution.py:130
  87.1 2.4 %shard_map.91 = (f32[2,256,256]{2,1,0:T(8,128)S(1)}, f32[2,256,256]{2,1,0:T(8,128)S(1)}, f32[1024,256]{1,0:T(8,128)S(1)}) custom-call(s32[5]{0:T(128)S(1)} %bitcast.45, s32[1]{0:T(128)} %bitcast.23.tile, bf16[5,1024,2048]{2,1,0:T(8,128)(2,1)S(1)} %copy-done.1, bf16[4,128,256]{2,1,0:T(8,128)(2,1)S(1)} %collective-permute-done.28.front, ...), custom_call_target="tpu_custom_call" | custom-call | flops 1342177280 | bytes 2621440 | tf_op jit(solution)/shard_map/pallas_call | solution.py:130
  90.2 1.6 collective-permute-start.15
  91.9 1.4 collective-permute-start.31
  93.3 3.5 %collective-permute-done.15.got = s16[272,256]{1,0:T(8,128)(2,1)S(1)} collective-permute-done((s16[272,256]{1,0:T(8,128)(2,1)S(1)}, s16[272,256]{1,0:T(8,128)(2,1)S(1)}, u32[]{:S(2)}, u32[]{:S(2)}) %collective-permute-start.15) | collective-permute-done | bytes 139296 | tf_op jit(solution)/shard_map/ppermute | solution.py:263
  96.9 1.6 collective-permute-start.32
  98.9 3.2 %collective-permute-done.32.refs_1_ = bf16[256,256]{1,0:T(8,128)(2,1)S(1)} collective-permute-done((bf16[256,256]{1,0:T(8,128)(2,1)S(1)}, bf16[256,256]{1,0:T(8,128)(2,1)S(1)}, u32[]{:S(2)}, u32[]{:S(2)}) %collective-permute-start.32) | collective-permute-done | bytes 131104 | tf_op jit(solution)/shard_map/ppermute | solution.py:263
  102.2 1.6 collective-permute-start.44
  103.7 1.4 collective-permute-start.33
  105.2 1.5 collective-permute-start.34
  106.7 1.4 collective-permute-start.45
  108.1 3.0 %collective-permute-start.46 = (bf16[256,256]{1,0:T(8,128)(2,1)S(1)}, bf16[256,256]{1,0:T(8,128)(2,1)S(1)}, u32[]{:S(2)}, u32[]{:S(2)}) collective-permute-start(bf16[256,256]{1,0:T(8,128)(2,1)S(1)} %collective-permute-done.44.refs_1_), channel_id=1, source_target_pairs={{0,16},{1,17},{2,18},{3,19},{4,20},{5,21},{6,22},{7,23},{8,24},{9,... | collective-permute-start | bytes 393224 | tf_op jit(solution)/shard_map/ppermute | solution.py:263
  111.1 8.5 %collective-permute-done.33.refs_2_ = bf16[256,256]{1,0:T(8,128)(2,1)S(1)} collective-permute-done((bf16[256,256]{1,0:T(8,128)(2,1)S(1)}, bf16[256,256]{1,0:T(8,128)(2,1)S(1)}, u32[]{:S(2)}, u32[]{:S(2)}) %collective-permute-start.33) | collective-permute-done | bytes 131104 | tf_op jit(solution)/shard_map/ppermute | solution.py:263
  119.6 2.8 %collective-permute-done.34.refs_3_ = bf16[256,256]{1,0:T(8,128)(2,1)S(1)} collective-permute-done((bf16[256,256]{1,0:T(8,128)(2,1)S(1)}, bf16[256,256]{1,0:T(8,128)(2,1)S(1)}, u32[]{:S(2)}, u32[]{:S(2)}) %collective-permute-start.34) | collective-permute-done | bytes 131104 | tf_op jit(solution)/shard_map/ppermute | solution.py:263
  122.6 1.6 collective-permute-start.36
  126.3 1.6 collective-permute-start.40
  129.4 1.5 collective-permute-done.37.refs_3_
  131.4 1.5 collective-permute-start.48
  133.2 4.6 %collective-permute-done.40.refs_6_ = bf16[256,256]{1,0:T(8,128)(2,1)S(1)} collective-permute-done((bf16[256,256]{1,0:T(8,128)(2,1)S(1)}, bf16[256,256]{1,0:T(8,128)(2,1)S(1)}, u32[]{:S(2)}, u32[]{:S(2)}) %collective-permute-start.40) | collective-permute-done | bytes 131104 | tf_op jit(solution)/shard_map/ppermute | solution.py:263
  138.7 1.8 %collective-permute-start.49 = (bf16[256,256]{1,0:T(8,128)(2,1)S(1)}, bf16[256,256]{1,0:T(8,128)(2,1)S(1)}, u32[]{:S(2)}, u32[]{:S(2)}) collective-permute-start(bf16[256,256]{1,0:T(8,128)(2,1)S(1)} %get-tuple-element.189), channel_id=1, source_target_pairs={{0,3},{1,2},{2,1},{3,0},{4,7},{5,6},{6,5},{7,4},{8,11},{9,10},{10,... | collective-permute-start | bytes 393224 | tf_op jit(solution)/shard_map/ppermute | solution.py:263
  141.0 1.9 %collective-permute-done.48.refs_2_ = bf16[256,256]{1,0:T(8,128)(2,1)S(1)} collective-permute-done((bf16[256,256]{1,0:T(8,128)(2,1)S(1)}, bf16[256,256]{1,0:T(8,128)(2,1)S(1)}, u32[]{:S(2)}, u32[]{:S(2)}) %collective-permute-start.48) | collective-permute-done | bytes 131104 | tf_op jit(solution)/shard_map/ppermute | solution.py:263
  143.3 2.3 %shard_map.95 = (f32[2,256,256]{2,1,0:T(8,128)S(1)}, f32[2,256,256]{2,1,0:T(8,128)S(1)}) custom-call(s32[5]{0:T(128)S(1)} %bitcast.46, s32[1]{0:T(128)} %bitcast.24.tile, bf16[5,1024,2048]{2,1,0:T(8,128)(2,1)S(1)} %copy-done.1, bf16[256,256]{1,0:T(8,128)(2,1)S(1)} %get-tuple-element.176.refs_0_, bf16[256,256]{1,0:T(8,128)(2,1)S(1)} %collective-permute-done.35.refs_1_, ...), custom_call_target="tpu_custom_call" | custom-call | flops 5368709120 | bytes 20971520 | tf_op jit(solution)/shard_map/pallas_call | solution.py:236
  145.6 4.1 %collective-permute-done.49.refs_3_ = bf16[256,256]{1,0:T(8,128)(2,1)S(1)} collective-permute-done((bf16[256,256]{1,0:T(8,128)(2,1)S(1)}, bf16[256,256]{1,0:T(8,128)(2,1)S(1)}, u32[]{:S(2)}, u32[]{:S(2)}) %collective-permute-start.49) | collective-permute-done | bytes 131104 | tf_op jit(solution)/shard_map/ppermute | solution.py:263
  150.2 2.2 %shard_map.99 = (f32[2,256,256]{2,1,0:T(8,128)S(1)}, f32[2,256,256]{2,1,0:T(8,128)S(1)}) custom-call(s32[5]{0:T(128)S(1)} %bitcast.47, s32[1]{0:T(128)} %bitcast.25.tile, bf16[5,1024,2048]{2,1,0:T(8,128)(2,1)S(1)} %copy-done.1, bf16[256,256]{1,0:T(8,128)(2,1)S(1)} %get-tuple-element.186.refs_0_, bf16[256,256]{1,0:T(8,128)(2,1)S(1)} %collective-permute-done.47.refs_1_, ...), custom_call_target="tpu_custom_call" | custom-call | flops 5368709120 | bytes 20971520 | tf_op jit(solution)/shard_map/pallas_call | solution.py:236
  152.6 3.9 %collective-permute-start.43 = (s16[272,256]{1,0:T(8,128)(2,1)S(1)}, s16[272,256]{1,0:T(8,128)(2,1)S(1)}, u32[]{:S(2)}, u32[]{:S(2)}) collective-permute-start(s16[272,256]{1,0:T(8,128)(2,1)S(1)} %get-tuple-element.184), channel_id=1, source_target_pairs={{0,2},{1,3},{2,0},{3,1},{4,6},{5,7},{6,4},{7,5},{8,10},{9,11},{10,... | collective-permute-start | bytes 417800 | tf_op jit(solution)/shard_map/ppermute | solution.py:263
  156.5 1.8 %collective-permute-start.55 = (s16[272,256]{1,0:T(8,128)(2,1)S(1)}, s16[272,256]{1,0:T(8,128)(2,1)S(1)}, u32[]{:S(2)}, u32[]{:S(2)}) collective-permute-start(s16[272,256]{1,0:T(8,128)(2,1)S(1)} %get-tuple-element.194), channel_id=1, source_target_pairs={{0,2},{1,3},{2,0},{3,1},{4,6},{5,7},{6,4},{7,5},{8,10},{9,11},{10,... | collective-permute-start | bytes 417800 | tf_op jit(solution)/shard_map/ppermute | solution.py:263
  158.3 2.7 %collective-permute-done.43.got = s16[272,256]{1,0:T(8,128)(2,1)S(1)} collective-permute-done((s16[272,256]{1,0:T(8,128)(2,1)S(1)}, s16[272,256]{1,0:T(8,128)(2,1)S(1)}, u32[]{:S(2)}, u32[]{:S(2)}) %collective-permute-start.43) | collective-permute-done | bytes 139296 | tf_op jit(solution)/shard_map/ppermute | solution.py:263
  161.1 2.7 %collective-permute-done.55.got = s16[272,256]{1,0:T(8,128)(2,1)S(1)} collective-permute-done((s16[272,256]{1,0:T(8,128)(2,1)S(1)}, s16[272,256]{1,0:T(8,128)(2,1)S(1)}, u32[]{:S(2)}, u32[]{:S(2)}) %collective-permute-start.55) | collective-permute-done | bytes 139296 | tf_op jit(solution)/shard_map/ppermute | solution.py:263
  (92 shorter events, 20.9 us)
Async XLA Ops:
  0.0 6.4 %copy-start.3 = (f32[1024]{0:T(1024)S(1)}, f32[1024]{0:T(1024)}, u32[]{:S(2)}) copy-start(f32[1024]{0:T(1024)} %param.10) | copy-start | bytes 12292
  0.0 6.4 %copy-start.4 = (f32[1024]{0:T(1024)S(1)}, f32[1024]{0:T(1024)}, u32[]{:S(2)}) copy-start(f32[1024]{0:T(1024)} %param.11) | copy-start | bytes 12292
  1.3 12.5 %collective-permute-start = (bf16[4,128,256]{2,1,0:T(8,128)(2,1)S(1)}, bf16[4,128,256]{2,1,0:T(8,128)(2,1)S(1)}, u32[]{:S(2)}, u32[]{:S(2)}) collective-permute-start(bf16[4,128,256]{2,1,0:T(8,128)(2,1)S(1)} %get-tuple-element.198.front), channel_id=1, source_target_pairs={{0,8},{4,0},{8,16},{12,4},{16,24},{20,12},{24,28},{28,20},{1,9},{5... | collective-permute-start | bytes 786440 | tf_op jit(solution)/shard_map/ppermute | solution.py:274
  4.4 9.4 %collective-permute-start.1 = (bf16[4,128,256]{2,1,0:T(8,128)(2,1)S(1)}, bf16[4,128,256]{2,1,0:T(8,128)(2,1)S(1)}, u32[]{:S(2)}, u32[]{:S(2)}) collective-permute-start(bf16[4,128,256]{2,1,0:T(8,128)(2,1)S(1)} %get-tuple-element.197.back), channel_id=1, source_target_pairs={{0,4},{4,12},{8,0},{12,20},{16,8},{20,28},{24,16},{28,24},{1,5},{5... | collective-permute-start | bytes 786440 | tf_op jit(solution)/shard_map/ppermute | solution.py:274
  4.4 12.6 %collective-permute-start.16 = (bf16[4,128,256]{2,1,0:T(8,128)(2,1)S(1)}, bf16[4,128,256]{2,1,0:T(8,128)(2,1)S(1)}, u32[]{:S(2)}, u32[]{:S(2)}) collective-permute-start(bf16[4,128,256]{2,1,0:T(8,128)(2,1)S(1)} %get-tuple-element.200.front), channel_id=1, source_target_pairs={{0,8},{4,0},{8,16},{12,4},{16,24},{20,12},{24,28},{28,20},{1,9},{5... | collective-permute-start | bytes 786440 | tf_op jit(solution)/shard_map/ppermute | solution.py:274
  6.4 12.2 %collective-permute-start.17 = (bf16[4,128,256]{2,1,0:T(8,128)(2,1)S(1)}, bf16[4,128,256]{2,1,0:T(8,128)(2,1)S(1)}, u32[]{:S(2)}, u32[]{:S(2)}) collective-permute-start(bf16[4,128,256]{2,1,0:T(8,128)(2,1)S(1)} %get-tuple-element.199.back), channel_id=1, source_target_pairs={{0,4},{4,12},{8,0},{12,20},{16,8},{20,28},{24,16},{28,24},{1,5},{5... | collective-permute-start | bytes 786440 | tf_op jit(solution)/shard_map/ppermute | solution.py:274
  6.4 7.0 %copy-start = (bf16[5,1024,2048]{2,1,0:T(8,128)(2,1)S(1)}, bf16[5,1024,2048]{2,1,0:T(8,128)(2,1)}, u32[]{:S(2)}) copy-start(bf16[5,1024,2048]{2,1,0:T(8,128)(2,1)} %matrix.57) | copy-start | bytes 62914564
  13.4 7.9 %copy-start.1 = (bf16[5,1024,2048]{2,1,0:T(8,128)(2,1)S(1)}, bf16[5,1024,2048]{2,1,0:T(8,128)(2,1)}, u32[]{:S(2)}) copy-start(bf16[5,1024,2048]{2,1,0:T(8,128)(2,1)} %matrix.57) | copy-start | bytes 62914564
  13.4 7.9 %copy-start.2 = (s32[1,1,5]{2,1,0:T(1,128)S(1)}, s32[1,1,5]{2,1,0:T(1,128)}, u32[]{:S(2)}) copy-start(s32[1,1,5]{2,1,0:T(1,128)} %param.12) | copy-start | bytes 64
  13.8 9.6 %collective-permute-start.2 = (bf16[4,128,256]{2,1,0:T(8,128)(2,1)S(1)}, bf16[4,128,256]{2,1,0:T(8,128)(2,1)S(1)}, u32[]{:S(2)}, u32[]{:S(2)}) collective-permute-start(bf16[4,128,256]{2,1,0:T(8,128)(2,1)S(1)} %collective-permute-done.front), channel_id=1, source_target_pairs={{0,8},{4,0},{8,16},{12,4},{16,24},{20,12},{24,28},{28,20},{1,9},{5... | collective-permute-start | bytes 786440 | tf_op jit(solution)/shard_map/ppermute | solution.py:274
  15.9 9.2 %collective-permute-start.3 = (bf16[4,128,256]{2,1,0:T(8,128)(2,1)S(1)}, bf16[4,128,256]{2,1,0:T(8,128)(2,1)S(1)}, u32[]{:S(2)}, u32[]{:S(2)}) collective-permute-start(bf16[4,128,256]{2,1,0:T(8,128)(2,1)S(1)} %collective-permute-done.1.back), channel_id=1, source_target_pairs={{0,4},{4,12},{8,0},{12,20},{16,8},{20,28},{24,16},{28,24},{1,5},{5... | collective-permute-start | bytes 786440 | tf_op jit(solution)/shard_map/ppermute | solution.py:274
  18.6 10.6 %collective-permute-start.18 = (bf16[4,128,256]{2,1,0:T(8,128)(2,1)S(1)}, bf16[4,128,256]{2,1,0:T(8,128)(2,1)S(1)}, u32[]{:S(2)}, u32[]{:S(2)}) collective-permute-start(bf16[4,128,256]{2,1,0:T(8,128)(2,1)S(1)} %collective-permute-done.16.front), channel_id=1, source_target_pairs={{0,8},{4,0},{8,16},{12,4},{16,24},{20,12},{24,28},{28,20},{1,9},{5... | collective-permute-start | bytes 786440 | tf_op jit(solution)/shard_map/ppermute | solution.py:274
  20.2 10.6 %collective-permute-start.19 = (bf16[4,128,256]{2,1,0:T(8,128)(2,1)S(1)}, bf16[4,128,256]{2,1,0:T(8,128)(2,1)S(1)}, u32[]{:S(2)}, u32[]{:S(2)}) collective-permute-start(bf16[4,128,256]{2,1,0:T(8,128)(2,1)S(1)} %collective-permute-done.17.back), channel_id=1, source_target_pairs={{0,4},{4,12},{8,0},{12,20},{16,8},{20,28},{24,16},{28,24},{1,5},{5... | collective-permute-start | bytes 786440 | tf_op jit(solution)/shard_map/ppermute | solution.py:274
  25.1 11.9 %collective-permute-start.4 = (bf16[4,128,256]{2,1,0:T(8,128)(2,1)S(1)}, bf16[4,128,256]{2,1,0:T(8,128)(2,1)S(1)}, u32[]{:S(2)}, u32[]{:S(2)}) collective-permute-start(bf16[4,128,256]{2,1,0:T(8,128)(2,1)S(1)} %collective-permute-done.2.front), channel_id=1, source_target_pairs={{0,8},{4,0},{8,16},{12,4},{16,24},{20,12},{24,28},{28,20},{1,9},{5... | collective-permute-start | bytes 786440 | tf_op jit(solution)/shard_map/ppermute | solution.py:274
  26.7 10.4 %collective-permute-start.5 = (bf16[4,128,256]{2,1,0:T(8,128)(2,1)S(1)}, bf16[4,128,256]{2,1,0:T(8,128)(2,1)S(1)}, u32[]{:S(2)}, u32[]{:S(2)}) collective-permute-start(bf16[4,128,256]{2,1,0:T(8,128)(2,1)S(1)} %collective-permute-done.3.back), channel_id=1, source_target_pairs={{0,4},{4,12},{8,0},{12,20},{16,8},{20,28},{24,16},{28,24},{1,5},{5... | collective-permute-start | bytes 786440 | tf_op jit(solution)/shard_map/ppermute | solution.py:274
  30.7 12.7 %collective-permute-start.20 = (bf16[4,128,256]{2,1,0:T(8,128)(2,1)S(1)}, bf16[4,128,256]{2,1,0:T(8,128)(2,1)S(1)}, u32[]{:S(2)}, u32[]{:S(2)}) collective-permute-start(bf16[4,128,256]{2,1,0:T(8,128)(2,1)S(1)} %collective-permute-done.18.front), channel_id=1, source_target_pairs={{0,8},{4,0},{8,16},{12,4},{16,24},{20,12},{24,28},{28,20},{1,9},{5... | collective-permute-start | bytes 786440 | tf_op jit(solution)/shard_map/ppermute | solution.py:274
  32.3 11.2 %collective-permute-start.21 = (bf16[4,128,256]{2,1,0:T(8,128)(2,1)S(1)}, bf16[4,128,256]{2,1,0:T(8,128)(2,1)S(1)}, u32[]{:S(2)}, u32[]{:S(2)}) collective-permute-start(bf16[4,128,256]{2,1,0:T(8,128)(2,1)S(1)} %collective-permute-done.19.back), channel_id=1, source_target_pairs={{0,4},{4,12},{8,0},{12,20},{16,8},{20,28},{24,16},{28,24},{1,5},{5... | collective-permute-start | bytes 786440 | tf_op jit(solution)/shard_map/ppermute | solution.py:274
  37.1 10.6 %collective-permute-start.6 = (bf16[4,128,256]{2,1,0:T(8,128)(2,1)S(1)}, bf16[4,128,256]{2,1,0:T(8,128)(2,1)S(1)}, u32[]{:S(2)}, u32[]{:S(2)}) collective-permute-start(bf16[4,128,256]{2,1,0:T(8,128)(2,1)S(1)} %collective-permute-done.4.front), channel_id=1, source_target_pairs={{0,8},{4,0},{8,16},{12,4},{16,24},{20,12},{24,28},{28,20},{1,9},{5... | collective-permute-start | bytes 786440 | tf_op jit(solution)/shard_map/ppermute | solution.py:274
  38.7 9.2 %collective-permute-start.7 = (bf16[4,128,256]{2,1,0:T(8,128)(2,1)S(1)}, bf16[4,128,256]{2,1,0:T(8,128)(2,1)S(1)}, u32[]{:S(2)}, u32[]{:S(2)}) collective-permute-start(bf16[4,128,256]{2,1,0:T(8,128)(2,1)S(1)} %collective-permute-done.5.back), channel_id=1, source_target_pairs={{0,4},{4,12},{8,0},{12,20},{16,8},{20,28},{24,16},{28,24},{1,5},{5... | collective-permute-start | bytes 786440 | tf_op jit(solution)/shard_map/ppermute | solution.py:274
  43.5 9.3 %collective-permute-start.22 = (bf16[4,128,256]{2,1,0:T(8,128)(2,1)S(1)}, bf16[4,128,256]{2,1,0:T(8,128)(2,1)S(1)}, u32[]{:S(2)}, u32[]{:S(2)}) collective-permute-start(bf16[4,128,256]{2,1,0:T(8,128)(2,1)S(1)} %collective-permute-done.20.front), channel_id=1, source_target_pairs={{0,8},{4,0},{8,16},{12,4},{16,24},{20,12},{24,28},{28,20},{1,9},{5... | collective-permute-start | bytes 786440 | tf_op jit(solution)/shard_map/ppermute | solution.py:274
  45.1 9.2 %collective-permute-start.23 = (bf16[4,128,256]{2,1,0:T(8,128)(2,1)S(1)}, bf16[4,128,256]{2,1,0:T(8,128)(2,1)S(1)}, u32[]{:S(2)}, u32[]{:S(2)}) collective-permute-start(bf16[4,128,256]{2,1,0:T(8,128)(2,1)S(1)} %collective-permute-done.21.back), channel_id=1, source_target_pairs={{0,4},{4,12},{8,0},{12,20},{16,8},{20,28},{24,16},{28,24},{1,5},{5... | collective-permute-start | bytes 786440 | tf_op jit(solution)/shard_map/ppermute | solution.py:274
  47.9 10.6 %collective-permute-start.8 = (bf16[4,128,256]{2,1,0:T(8,128)(2,1)S(1)}, bf16[4,128,256]{2,1,0:T(8,128)(2,1)S(1)}, u32[]{:S(2)}, u32[]{:S(2)}) collective-permute-start(bf16[4,128,256]{2,1,0:T(8,128)(2,1)S(1)} %collective-permute-done.6.front), channel_id=1, source_target_pairs={{0,8},{4,0},{8,16},{12,4},{16,24},{20,12},{24,28},{28,20},{1,9},{5... | collective-permute-start | bytes 786440 | tf_op jit(solution)/shard_map/ppermute | solution.py:274
  49.5 10.4 %collective-permute-start.9 = (bf16[4,128,256]{2,1,0:T(8,128)(2,1)S(1)}, bf16[4,128,256]{2,1,0:T(8,128)(2,1)S(1)}, u32[]{:S(2)}, u32[]{:S(2)}) collective-permute-start(bf16[4,128,256]{2,1,0:T(8,128)(2,1)S(1)} %collective-permute-done.7.back), channel_id=1, source_target_pairs={{0,4},{4,12},{8,0},{12,20},{16,8},{20,28},{24,16},{28,24},{1,5},{5... | collective-permute-start | bytes 786440 | tf_op jit(solution)/shard_map/ppermute | solution.py:274
  54.3 9.8 %collective-permute-start.24 = (bf16[4,128,256]{2,1,0:T(8,128)(2,1)S(1)}, bf16[4,128,256]{2,1,0:T(8,128)(2,1)S(1)}, u32[]{:S(2)}, u32[]{:S(2)}) collective-permute-start(bf16[4,128,256]{2,1,0:T(8,128)(2,1)S(1)} %collective-permute-done.22.front), channel_id=1, source_target_pairs={{0,8},{4,0},{8,16},{12,4},{16,24},{20,12},{24,28},{28,20},{1,9},{5... | collective-permute-start | bytes 786440 | tf_op jit(solution)/shard_map/ppermute | solution.py:274
  55.9 9.7 %collective-permute-start.25 = (bf16[4,128,256]{2,1,0:T(8,128)(2,1)S(1)}, bf16[4,128,256]{2,1,0:T(8,128)(2,1)S(1)}, u32[]{:S(2)}, u32[]{:S(2)}) collective-permute-start(bf16[4,128,256]{2,1,0:T(8,128)(2,1)S(1)} %collective-permute-done.23.back), channel_id=1, source_target_pairs={{0,4},{4,12},{8,0},{12,20},{16,8},{20,28},{24,16},{28,24},{1,5},{5... | collective-permute-start | bytes 786440 | tf_op jit(solution)/shard_map/ppermute | solution.py:274
  60.0 9.8 %collective-permute-start.10 = (bf16[4,128,256]{2,1,0:T(8,128)(2,1)S(1)}, bf16[4,128,256]{2,1,0:T(8,128)(2,1)S(1)}, u32[]{:S(2)}, u32[]{:S(2)}) collective-permute-start(bf16[4,128,256]{2,1,0:T(8,128)(2,1)S(1)} %collective-permute-done.8.front), channel_id=1, source_target_pairs={{0,8},{4,0},{8,16},{12,4},{16,24},{20,12},{24,28},{28,20},{1,9},{5... | collective-permute-start | bytes 786440 | tf_op jit(solution)/shard_map/ppermute | solution.py:274
  61.5 9.7 %collective-permute-start.11 = (bf16[4,128,256]{2,1,0:T(8,128)(2,1)S(1)}, bf16[4,128,256]{2,1,0:T(8,128)(2,1)S(1)}, u32[]{:S(2)}, u32[]{:S(2)}) collective-permute-start(bf16[4,128,256]{2,1,0:T(8,128)(2,1)S(1)} %collective-permute-done.9.back), channel_id=1, source_target_pairs={{0,4},{4,12},{8,0},{12,20},{16,8},{20,28},{24,16},{28,24},{1,5},{5... | collective-permute-start | bytes 786440 | tf_op jit(solution)/shard_map/ppermute | solution.py:274
  65.6 9.9 %collective-permute-start.26 = (bf16[4,128,256]{2,1,0:T(8,128)(2,1)S(1)}, bf16[4,128,256]{2,1,0:T(8,128)(2,1)S(1)}, u32[]{:S(2)}, u32[]{:S(2)}) collective-permute-start(bf16[4,128,256]{2,1,0:T(8,128)(2,1)S(1)} %collective-permute-done.24.front), channel_id=1, source_target_pairs={{0,8},{4,0},{8,16},{12,4},{16,24},{20,12},{24,28},{28,20},{1,9},{5... | collective-permute-start | bytes 786440 | tf_op jit(solution)/shard_map/ppermute | solution.py:274
  67.2 9.7 %collective-permute-start.27 = (bf16[4,128,256]{2,1,0:T(8,128)(2,1)S(1)}, bf16[4,128,256]{2,1,0:T(8,128)(2,1)S(1)}, u32[]{:S(2)}, u32[]{:S(2)}) collective-permute-start(bf16[4,128,256]{2,1,0:T(8,128)(2,1)S(1)} %collective-permute-done.25.back), channel_id=1, source_target_pairs={{0,4},{4,12},{8,0},{12,20},{16,8},{20,28},{24,16},{28,24},{1,5},{5... | collective-permute-start | bytes 786440 | tf_op jit(solution)/shard_map/ppermute | solution.py:274
  67.6 5.6 %copy-start.5 = (f32[2,256,512]{2,1,0:T(8,128)S(1)}, f32[2,256,512]{2,1,0:T(8,128)}, u32[]{:S(2)}) copy-start(f32[2,256,512]{2,1,0:T(8,128)} %param.9) | copy-start | bytes 3145732
  71.2 9.8 %collective-permute-start.12 = (bf16[4,128,256]{2,1,0:T(8,128)(2,1)S(1)}, bf16[4,128,256]{2,1,0:T(8,128)(2,1)S(1)}, u32[]{:S(2)}, u32[]{:S(2)}) collective-permute-start(bf16[4,128,256]{2,1,0:T(8,128)(2,1)S(1)} %collective-permute-done.10.front), channel_id=1, source_target_pairs={{0,8},{4,0},{8,16},{12,4},{16,24},{20,12},{24,28},{28,20},{1,9},{5... | collective-permute-start | bytes 786440 | tf_op jit(solution)/shard_map/ppermute | solution.py:274
  72.8 9.6 %collective-permute-start.13 = (bf16[4,128,256]{2,1,0:T(8,128)(2,1)S(1)}, bf16[4,128,256]{2,1,0:T(8,128)(2,1)S(1)}, u32[]{:S(2)}, u32[]{:S(2)}) collective-permute-start(bf16[4,128,256]{2,1,0:T(8,128)(2,1)S(1)} %collective-permute-done.11.back), channel_id=1, source_target_pairs={{0,4},{4,12},{8,0},{12,20},{16,8},{20,28},{24,16},{28,24},{1,5},{5... | collective-permute-start | bytes 786440 | tf_op jit(solution)/shard_map/ppermute | solution.py:274
  76.8 10.2 %collective-permute-start.28 = (bf16[4,128,256]{2,1,0:T(8,128)(2,1)S(1)}, bf16[4,128,256]{2,1,0:T(8,128)(2,1)S(1)}, u32[]{:S(2)}, u32[]{:S(2)}) collective-permute-start(bf16[4,128,256]{2,1,0:T(8,128)(2,1)S(1)} %collective-permute-done.26.front), channel_id=1, source_target_pairs={{0,8},{4,0},{8,16},{12,4},{16,24},{20,12},{24,28},{28,20},{1,9},{5... | collective-permute-start | bytes 786440 | tf_op jit(solution)/shard_map/ppermute | solution.py:274
  78.4 8.6 %collective-permute-start.29 = (bf16[4,128,256]{2,1,0:T(8,128)(2,1)S(1)}, bf16[4,128,256]{2,1,0:T(8,128)(2,1)S(1)}, u32[]{:S(2)}, u32[]{:S(2)}) collective-permute-start(bf16[4,128,256]{2,1,0:T(8,128)(2,1)S(1)} %collective-permute-done.27.back), channel_id=1, source_target_pairs={{0,4},{4,12},{8,0},{12,20},{16,8},{20,28},{24,16},{28,24},{1,5},{5... | collective-permute-start | bytes 786440 | tf_op jit(solution)/shard_map/ppermute | solution.py:274
  84.8 5.3 %collective-permute-start.14 = (f32[2,256,256]{2,1,0:T(8,128)S(1)}, f32[2,256,256]{2,1,0:T(8,128)S(1)}, u32[]{:S(2)}, u32[]{:S(2)}) collective-permute-start(f32[2,256,256]{2,1,0:T(8,128)S(1)} %get-tuple-element.134), channel_id=1, source_target_pairs={{0,1},{1,0},{2,3},{3,2},{4,5},{5,4},{6,7},{7,6},{8,9},{9,8},{10,11... | collective-permute-start | bytes 1572872 | tf_op jit(solution)/shard_map/ppermute | solution.py:263
  89.5 2.3 %collective-permute-start.30 = (f32[2,256,256]{2,1,0:T(8,128)S(1)}, f32[2,256,256]{2,1,0:T(8,128)S(1)}, u32[]{:S(2)}, u32[]{:S(2)}) collective-permute-start(f32[2,256,256]{2,1,0:T(8,128)S(1)} %get-tuple-element.172), channel_id=1, source_target_pairs={{0,1},{1,0},{2,3},{3,2},{4,5},{5,4},{6,7},{7,6},{8,9},{9,8},{10,11... | collective-permute-start | bytes 1572872 | tf_op jit(solution)/shard_map/ppermute | solution.py:263
  90.2 6.6 %collective-permute-start.15 = (s16[272,256]{1,0:T(8,128)(2,1)S(1)}, s16[272,256]{1,0:T(8,128)(2,1)S(1)}, u32[]{:S(2)}, u32[]{:S(2)}) collective-permute-start(s16[272,256]{1,0:T(8,128)(2,1)S(1)} %get-tuple-element.136), channel_id=1, source_target_pairs={{0,2},{1,3},{2,0},{3,1},{4,6},{5,7},{6,4},{7,5},{8,10},{9,11},{10,... | collective-permute-start | bytes 417800 | tf_op jit(solution)/shard_map/ppermute | solution.py:263
  91.9 7.0 %collective-permute-start.31 = (s16[272,256]{1,0:T(8,128)(2,1)S(1)}, s16[272,256]{1,0:T(8,128)(2,1)S(1)}, u32[]{:S(2)}, u32[]{:S(2)}) collective-permute-start(s16[272,256]{1,0:T(8,128)(2,1)S(1)} %get-tuple-element.174), channel_id=1, source_target_pairs={{0,2},{1,3},{2,0},{3,1},{4,6},{5,7},{6,4},{7,5},{8,10},{9,11},{10,... | collective-permute-start | bytes 417800 | tf_op jit(solution)/shard_map/ppermute | solution.py:263
  96.9 5.3 %collective-permute-start.32 = (bf16[256,256]{1,0:T(8,128)(2,1)S(1)}, bf16[256,256]{1,0:T(8,128)(2,1)S(1)}, u32[]{:S(2)}, u32[]{:S(2)}) collective-permute-start(bf16[256,256]{1,0:T(8,128)(2,1)S(1)} %shard_map.83.refs_0_), channel_id=1, source_target_pairs={{0,8},{1,9},{2,10},{3,11},{4,12},{5,13},{6,14},{7,15},{8,0},{9,1},... | collective-permute-start | bytes 393224 | tf_op jit(solution)/shard_map/ppermute | solution.py:263
  102.2 5.9 %collective-permute-start.44 = (bf16[256,256]{1,0:T(8,128)(2,1)S(1)}, bf16[256,256]{1,0:T(8,128)(2,1)S(1)}, u32[]{:S(2)}, u32[]{:S(2)}) collective-permute-start(bf16[256,256]{1,0:T(8,128)(2,1)S(1)} %shard_map.93.refs_0_), channel_id=1, source_target_pairs={{0,8},{1,9},{2,10},{3,11},{4,12},{5,13},{6,14},{7,15},{8,0},{9,1},... | collective-permute-start | bytes 393224 | tf_op jit(solution)/shard_map/ppermute | solution.py:263
  103.7 15.9 %collective-permute-start.33 = (bf16[256,256]{1,0:T(8,128)(2,1)S(1)}, bf16[256,256]{1,0:T(8,128)(2,1)S(1)}, u32[]{:S(2)}, u32[]{:S(2)}) collective-permute-start(bf16[256,256]{1,0:T(8,128)(2,1)S(1)} %shard_map.83.refs_0_), channel_id=1, source_target_pairs={{0,16},{1,17},{2,18},{3,19},{4,20},{5,21},{6,22},{7,23},{8,24},{9,... | collective-permute-start | bytes 393224 | tf_op jit(solution)/shard_map/ppermute | solution.py:263
  105.2 17.3 %collective-permute-start.34 = (bf16[256,256]{1,0:T(8,128)(2,1)S(1)}, bf16[256,256]{1,0:T(8,128)(2,1)S(1)}, u32[]{:S(2)}, u32[]{:S(2)}) collective-permute-start(bf16[256,256]{1,0:T(8,128)(2,1)S(1)} %collective-permute-done.32.refs_1_), channel_id=1, source_target_pairs={{0,16},{1,17},{2,18},{3,19},{4,20},{5,21},{6,22},{7,23},{8,24},{9,... | collective-permute-start | bytes 393224 | tf_op jit(solution)/shard_map/ppermute | solution.py:263
  106.7 18.2 %collective-permute-start.45 = (bf16[256,256]{1,0:T(8,128)(2,1)S(1)}, bf16[256,256]{1,0:T(8,128)(2,1)S(1)}, u32[]{:S(2)}, u32[]{:S(2)}) collective-permute-start(bf16[256,256]{1,0:T(8,128)(2,1)S(1)} %shard_map.93.refs_0_), channel_id=1, source_target_pairs={{0,16},{1,17},{2,18},{3,19},{4,20},{5,21},{6,22},{7,23},{8,24},{9,... | collective-permute-start | bytes 393224 | tf_op jit(solution)/shard_map/ppermute | solution.py:263
  108.1 18.2 %collective-permute-start.46 = (bf16[256,256]{1,0:T(8,128)(2,1)S(1)}, bf16[256,256]{1,0:T(8,128)(2,1)S(1)}, u32[]{:S(2)}, u32[]{:S(2)}) collective-permute-start(bf16[256,256]{1,0:T(8,128)(2,1)S(1)} %collective-permute-done.44.refs_1_), channel_id=1, source_target_pairs={{0,16},{1,17},{2,18},{3,19},{4,20},{5,21},{6,22},{7,23},{8,24},{9,... | collective-permute-start | bytes 393224 | tf_op jit(solution)/shard_map/ppermute | solution.py:263
  122.5 3.8 %collective-permute-start.35 = (bf16[256,256]{1,0:T(8,128)(2,1)S(1)}, bf16[256,256]{1,0:T(8,128)(2,1)S(1)}, u32[]{:S(2)}, u32[]{:S(2)}) collective-permute-start(bf16[256,256]{1,0:T(8,128)(2,1)S(1)} %get-tuple-element.177), channel_id=1, source_target_pairs={{0,1},{1,0},{2,3},{3,2},{4,5},{5,4},{6,7},{7,6},{8,9},{9,8},{10,11... | collective-permute-start | bytes 393224 | tf_op jit(solution)/shard_map/ppermute | solution.py:263
  122.6 6.4 %collective-permute-start.36 = (bf16[256,256]{1,0:T(8,128)(2,1)S(1)}, bf16[256,256]{1,0:T(8,128)(2,1)S(1)}, u32[]{:S(2)}, u32[]{:S(2)}) collective-permute-start(bf16[256,256]{1,0:T(8,128)(2,1)S(1)} %get-tuple-element.178), channel_id=1, source_target_pairs={{0,2},{1,3},{2,0},{3,1},{4,6},{5,7},{6,4},{7,5},{8,10},{9,11},{10,... | collective-permute-start | bytes 393224 | tf_op jit(solution)/shard_map/ppermute | solution.py:263
  124.2 6.7 %collective-permute-start.37 = (bf16[256,256]{1,0:T(8,128)(2,1)S(1)}, bf16[256,256]{1,0:T(8,128)(2,1)S(1)}, u32[]{:S(2)}, u32[]{:S(2)}) collective-permute-start(bf16[256,256]{1,0:T(8,128)(2,1)S(1)} %get-tuple-element.179), channel_id=1, source_target_pairs={{0,3},{1,2},{2,1},{3,0},{4,7},{5,6},{6,5},{7,4},{8,11},{9,10},{10,... | collective-permute-start | bytes 393224 | tf_op jit(solution)/shard_map/ppermute | solution.py:263
  124.9 6.5 %collective-permute-start.38 = (bf16[256,256]{1,0:T(8,128)(2,1)S(1)}, bf16[256,256]{1,0:T(8,128)(2,1)S(1)}, u32[]{:S(2)}, u32[]{:S(2)}) collective-permute-start(bf16[256,256]{1,0:T(8,128)(2,1)S(1)} %get-tuple-element.176.refs_0_), channel_id=1, source_target_pairs={{0,4},{1,5},{2,6},{3,7},{4,0},{5,1},{6,2},{7,3},{8,12},{9,13},{10,... | collective-permute-start | bytes 393224 | tf_op jit(solution)/shard_map/ppermute | solution.py:263
  126.3 6.7 %collective-permute-start.39 = (bf16[256,256]{1,0:T(8,128)(2,1)S(1)}, bf16[256,256]{1,0:T(8,128)(2,1)S(1)}, u32[]{:S(2)}, u32[]{:S(2)}) collective-permute-start(bf16[256,256]{1,0:T(8,128)(2,1)S(1)} %get-tuple-element.177), channel_id=1, source_target_pairs={{0,5},{1,4},{2,7},{3,6},{4,1},{5,0},{6,3},{7,2},{8,13},{9,12},{10,... | collective-permute-start | bytes 393224 | tf_op jit(solution)/shard_map/ppermute | solution.py:263
  126.3 11.5 %collective-permute-start.40 = (bf16[256,256]{1,0:T(8,128)(2,1)S(1)}, bf16[256,256]{1,0:T(8,128)(2,1)S(1)}, u32[]{:S(2)}, u32[]{:S(2)}) collective-permute-start(bf16[256,256]{1,0:T(8,128)(2,1)S(1)} %get-tuple-element.178), channel_id=1, source_target_pairs={{0,6},{1,7},{2,4},{3,5},{4,2},{5,3},{6,0},{7,1},{8,14},{9,15},{10,... | collective-permute-start | bytes 393224 | tf_op jit(solution)/shard_map/ppermute | solution.py:263
  128.9 9.8 %collective-permute-start.41 = (bf16[256,256]{1,0:T(8,128)(2,1)S(1)}, bf16[256,256]{1,0:T(8,128)(2,1)S(1)}, u32[]{:S(2)}, u32[]{:S(2)}) collective-permute-start(bf16[256,256]{1,0:T(8,128)(2,1)S(1)} %get-tuple-element.179), channel_id=1, source_target_pairs={{0,7},{1,6},{2,5},{3,4},{4,3},{5,2},{6,1},{7,0},{8,15},{9,14},{10,... | collective-permute-start | bytes 393224 | tf_op jit(solution)/shard_map/ppermute | solution.py:263
  130.8 9.7 %collective-permute-start.47 = (bf16[256,256]{1,0:T(8,128)(2,1)S(1)}, bf16[256,256]{1,0:T(8,128)(2,1)S(1)}, u32[]{:S(2)}, u32[]{:S(2)}) collective-permute-start(bf16[256,256]{1,0:T(8,128)(2,1)S(1)} %get-tuple-element.187), channel_id=1, source_target_pairs={{0,1},{1,0},{2,3},{3,2},{4,5},{5,4},{6,7},{7,6},{8,9},{9,8},{10,11... | collective-permute-start | bytes 393224 | tf_op jit(solution)/shard_map/ppermute | solution.py:263
  131.4 11.5 %collective-permute-start.48 = (bf16[256,256]{1,0:T(8,128)(2,1)S(1)}, bf16[256,256]{1,0:T(8,128)(2,1)S(1)}, u32[]{:S(2)}, u32[]{:S(2)}) collective-permute-start(bf16[256,256]{1,0:T(8,128)(2,1)S(1)} %get-tuple-element.188), channel_id=1, source_target_pairs={{0,2},{1,3},{2,0},{3,1},{4,6},{5,7},{6,4},{7,5},{8,10},{9,11},{10,... | collective-permute-start | bytes 393224 | tf_op jit(solution)/shard_map/ppermute | solution.py:263
  132.9 17.2 %collective-permute-start.51 = (bf16[256,256]{1,0:T(8,128)(2,1)S(1)}, bf16[256,256]{1,0:T(8,128)(2,1)S(1)}, u32[]{:S(2)}, u32[]{:S(2)}) collective-permute-start(bf16[256,256]{1,0:T(8,128)(2,1)S(1)} %get-tuple-element.187), channel_id=1, source_target_pairs={{0,5},{1,4},{2,7},{3,6},{4,1},{5,0},{6,3},{7,2},{8,13},{9,12},{10,... | collective-permute-start | bytes 393224 | tf_op jit(solution)/shard_map/ppermute | solution.py:263
  137.8 12.4 %collective-permute-start.52 = (bf16[256,256]{1,0:T(8,128)(2,1)S(1)}, bf16[256,256]{1,0:T(8,128)(2,1)S(1)}, u32[]{:S(2)}, u32[]{:S(2)}) collective-permute-start(bf16[256,256]{1,0:T(8,128)(2,1)S(1)} %get-tuple-element.188), channel_id=1, source_target_pairs={{0,6},{1,7},{2,4},{3,5},{4,2},{5,3},{6,0},{7,1},{8,14},{9,15},{10,... | collective-permute-start | bytes 393224 | tf_op jit(solution)/shard_map/ppermute | solution.py:263
  138.7 11.0 %collective-permute-start.49 = (bf16[256,256]{1,0:T(8,128)(2,1)S(1)}, bf16[256,256]{1,0:T(8,128)(2,1)S(1)}, u32[]{:S(2)}, u32[]{:S(2)}) collective-permute-start(bf16[256,256]{1,0:T(8,128)(2,1)S(1)} %get-tuple-element.189), channel_id=1, source_target_pairs={{0,3},{1,2},{2,1},{3,0},{4,7},{5,6},{6,5},{7,4},{8,11},{9,10},{10,... | collective-permute-start | bytes 393224 | tf_op jit(solution)/shard_map/ppermute | solution.py:263
  140.5 9.7 %collective-permute-start.53 = (bf16[256,256]{1,0:T(8,128)(2,1)S(1)}, bf16[256,256]{1,0:T(8,128)(2,1)S(1)}, u32[]{:S(2)}, u32[]{:S(2)}) collective-permute-start(bf16[256,256]{1,0:T(8,128)(2,1)S(1)} %get-tuple-element.189), channel_id=1, source_target_pairs={{0,7},{1,6},{2,5},{3,4},{4,3},{5,2},{6,1},{7,0},{8,15},{9,14},{10,... | collective-permute-start | bytes 393224 | tf_op jit(solution)/shard_map/ppermute | solution.py:263
  142.9 7.3 %collective-permute-start.50 = (bf16[256,256]{1,0:T(8,128)(2,1)S(1)}, bf16[256,256]{1,0:T(8,128)(2,1)S(1)}, u32[]{:S(2)}, u32[]{:S(2)}) collective-permute-start(bf16[256,256]{1,0:T(8,128)(2,1)S(1)} %get-tuple-element.186.refs_0_), channel_id=1, source_target_pairs={{0,4},{1,5},{2,6},{3,7},{4,0},{5,1},{6,2},{7,3},{8,12},{9,13},{10,... | collective-permute-start | bytes 393224 | tf_op jit(solution)/shard_map/ppermute | solution.py:263
  149.7 2.8 %collective-permute-start.42 = (f32[2,256,256]{2,1,0:T(8,128)S(1)}, f32[2,256,256]{2,1,0:T(8,128)S(1)}, u32[]{:S(2)}, u32[]{:S(2)}) collective-permute-start(f32[2,256,256]{2,1,0:T(8,128)S(1)} %get-tuple-element.182), channel_id=1, source_target_pairs={{0,1},{1,0},{2,3},{3,2},{4,5},{5,4},{6,7},{7,6},{8,9},{9,8},{10,11... | collective-permute-start | bytes 1572872 | tf_op jit(solution)/shard_map/ppermute | solution.py:263
  152.4 4.1 %collective-permute-start.54 = (f32[2,256,256]{2,1,0:T(8,128)S(1)}, f32[2,256,256]{2,1,0:T(8,128)S(1)}, u32[]{:S(2)}, u32[]{:S(2)}) collective-permute-start(f32[2,256,256]{2,1,0:T(8,128)S(1)} %get-tuple-element.192), channel_id=1, source_target_pairs={{0,1},{1,0},{2,3},{3,2},{4,5},{5,4},{6,7},{7,6},{8,9},{9,8},{10,11... | collective-permute-start | bytes 1572872 | tf_op jit(solution)/shard_map/ppermute | solution.py:263
  152.6 8.4 %collective-permute-start.43 = (s16[272,256]{1,0:T(8,128)(2,1)S(1)}, s16[272,256]{1,0:T(8,128)(2,1)S(1)}, u32[]{:S(2)}, u32[]{:S(2)}) collective-permute-start(s16[272,256]{1,0:T(8,128)(2,1)S(1)} %get-tuple-element.184), channel_id=1, source_target_pairs={{0,2},{1,3},{2,0},{3,1},{4,6},{5,7},{6,4},{7,5},{8,10},{9,11},{10,... | collective-permute-start | bytes 417800 | tf_op jit(solution)/shard_map/ppermute | solution.py:263
  156.5 7.2 %collective-permute-start.55 = (s16[272,256]{1,0:T(8,128)(2,1)S(1)}, s16[272,256]{1,0:T(8,128)(2,1)S(1)}, u32[]{:S(2)}, u32[]{:S(2)}) collective-permute-start(s16[272,256]{1,0:T(8,128)(2,1)S(1)} %get-tuple-element.194), channel_id=1, source_target_pairs={{0,2},{1,3},{2,0},{3,1},{4,6},{5,7},{6,4},{7,5},{8,10},{9,11},{10,... | collective-permute-start | bytes 417800 | tf_op jit(solution)/shard_map/ppermute | solution.py:263
